TPU v7x, 512 devices: a whole 4x8x8 slice. The times are simulated.
512 devices in a mesh: dp: 32 (over x, y), tensor: 16 (over z, core).
Axes of the slice: x: 4, y: 8, z: 8, core: 2. Of those that a mesh axis runs over, the one named last changes fastest.
Arguments:
- normed: bfloat16 [32768, 1536], P('dp', 'tensor'), may hold values from -6 to 6
- cotangent: bfloat16 [32768, 6144], P('dp', 'tensor'), may hold values from -6 to 6
- weight: bfloat16 [1536, 6144], P(None, 'tensor'), may hold values from -0.15625 to 0.15625
- error: bfloat16 [32, 1536, 6144], P('dp', None, 'tensor'), may hold values from -48 to 48
- q_init: float32 [32, 6144], P(None, 'tensor'), may hold values from -6 to 6
- lengths: int32 [128], P('dp'), may hold values from 64 to 256
- film_scale: float32 [128, 1536], P('dp'), may hold values from 0.1 to 1.9
- film_shift: float32 [128, 1536], P('dp'), may hold values from -3 to 3
Outputs:
- d_normed: bfloat16 [32768, 1536], P('dp', 'tensor')
- d_scale: float32 [128, 1536], P('dp', 'tensor')
- d_shift: float32 [128, 1536], P('dp', 'tensor')
- p_factor: float32 [16, 32, 1536], P('tensor')
- q_next: float32 [32, 6144], P(None, 'tensor')
- new_error: bfloat16 [32, 1536, 6144], P('dp', None, 'tensor')
All inputs are finite; a program needn't handle non-finite values.
Results may differ from a plain program's by a relative error of at most 0.023.
Values may be sent and summed in bfloat16 or wider, within the bound.
No kernel may reach another device: no remote copies, remote signals or barrier semaphores. Data moves between devices by JAX's collectives and lax.ppermute only.
A program may use at most 64 MiB of HBM per device.

v0:
```python
import jax
import jax.numpy as jnp
from jax import lax
from jax.sharding import PartitionSpec as P

SEQ = 256


def gelu_slope(u):
    cdf = 0.5 * (1.0 + lax.erf(u * 0.7071067811865476))
    dens = jnp.exp(-0.5 * u * u) * 0.3989422804014327
    return cdf + u * dens


def orthonormal(pmat):

    def one_column(j, basis):
        column = lax.dynamic_slice_in_dim(pmat, j, 1, 1)
        coeffs = jnp.dot(basis.T, column, precision=lax.Precision.HIGHEST)
        column = column - jnp.dot(basis, coeffs, precision=lax.Precision.HIGHEST)
        column = column / (jnp.sqrt(jnp.sum(column * column)) + 1e-06)
        return lax.dynamic_update_slice_in_dim(basis, column, j, 1)

    return lax.fori_loop(0, pmat.shape[1], one_column, jnp.zeros_like(pmat))


def sample_table(row_index, samp_count):
    return (row_index[:, None] // SEQ == jnp.arange(samp_count, dtype=jnp.int32)[None, :]).astype(
        jnp.float32
    )


def local(normed, cotangent, weight, error, q_init, lengths, film_scale, film_shift):
    samp_count = lengths.shape[0]
    col_width = normed.shape[1]
    tok_rows = cotangent.shape[0]
    rows = lax.all_gather(normed, "tensor", axis=1, tiled=True)
    position = jnp.arange(tok_rows, dtype=jnp.int32)
    onehot = sample_table(position, samp_count)
    scale_rows = jnp.dot(onehot, film_scale, precision=lax.Precision.HIGHEST)
    shift_rows = jnp.dot(onehot, film_shift, precision=lax.Precision.HIGHEST)
    limit_rows = jnp.sum(onehot.astype(jnp.int32) * lengths[None, :], axis=1)
    valid = (position % SEQ < limit_rows).astype(jnp.float32)
    z_rows = (rows.astype(jnp.float32) * scale_rows + shift_rows).astype(jnp.bfloat16)
    u = jnp.dot(z_rows, weight, preferred_element_type=jnp.float32)
    d_pre = (cotangent.astype(jnp.float32) * gelu_slope(u) * valid[:, None]).astype(jnp.bfloat16)
    moment = lax.dot_general(
        z_rows, d_pre, (((0,), (0,)), ((), ())), preferred_element_type=jnp.float32
    )
    moment = moment + error[0].astype(jnp.float32)
    col_start = lax.axis_index("tensor") * col_width
    own_scale = lax.dynamic_slice_in_dim(scale_rows, col_start, col_width, 1)
    partial_value = lax.dot_general(
        d_pre, weight, (((1,), (1,)), ((), ())), preferred_element_type=jnp.float32
    )
    partial_value = partial_value.astype(jnp.bfloat16).astype(jnp.float32)
    scale_full = jnp.dot(
        onehot.T, partial_value * rows.astype(jnp.float32), precision=lax.Precision.HIGHEST
    )
    shift_full = jnp.dot(onehot.T, partial_value, precision=lax.Precision.HIGHEST)
    d_scale, d_shift = (
        lax.psum_scatter(
            scale_full.astype(jnp.bfloat16), "tensor", scatter_dimension=1, tiled=True
        ).astype(jnp.float32),
        lax.psum_scatter(
            shift_full.astype(jnp.bfloat16), "tensor", scatter_dimension=1, tiled=True
        ).astype(jnp.float32),
    )
    dz = lax.psum_scatter(
        partial_value.astype(jnp.bfloat16), "tensor", scatter_dimension=1, tiled=True
    ).astype(jnp.float32)
    d_normed = (dz * own_scale).astype(jnp.bfloat16)
    p_local = lax.dot_general(
        moment, q_init, (((1,), (1,)), ((), ())), precision=lax.Precision.HIGHEST
    )
    p_total = lax.psum(p_local.astype(jnp.bfloat16), "dp").astype(jnp.float32)
    p_hat = orthonormal(p_total)
    q_local = lax.dot_general(
        p_hat, moment, (((0,), (0,)), ((), ())), precision=lax.Precision.HIGHEST
    )
    q_new = lax.psum(q_local.astype(jnp.bfloat16), "dp").astype(jnp.float32) / lax.axis_size("dp")
    averaged = jnp.dot(p_hat, q_new, precision=lax.Precision.HIGHEST)
    new_error = (moment - averaged).astype(jnp.bfloat16)[None]
    return (d_normed, d_scale, d_shift, p_hat.T[None], q_new, new_error)


def solution(mesh):
    return jax.shard_map(
        local,
        mesh=mesh,
        in_specs=(
            P("dp", "tensor"),
            P("dp", "tensor"),
            P(None, "tensor"),
            P("dp", None, "tensor"),
            P(None, "tensor"),
            P("dp"),
            P("dp", None),
            P("dp", None),
        ),
        out_specs=(
            P("dp", "tensor"),
            P("dp", "tensor"),
            P("dp", "tensor"),
            P("tensor", None, None),
            P(None, "tensor"),
            P("dp", None, "tensor"),
        ),
        check_vma=False,
    )
```

profile of v0, /device:TPU:64, one launch (start us, length us, event | category | flops | bytes accessed | tf_op | source)
XLA Modules:
  0.0 572.0 jit_solution(6028338248457752388)
XLA Ops:
  8.7 5.3 fusion.17
  14.1 43.8 %all-gather.2.cloned.1.call-done = bf16[1024,1536]{0,1:T(8,128)(2,1)} async-done(((bf16[1024,96]{0,1:T(8,128)(2,1)}), bf16[1024,1536]{0,1:T(8,128)(2,1)}) %all-gather.2.cloned.1.call-update) | async-done | bytes 3145744 | tf_op jit(solution)/shard_map/all_gather | solution.py:37
  57.9 4.6 copy.22
  62.5 5.7 fusion.4
  68.2 2.3 fusion.16
  70.5 1.8 convolution_convert_fusion
  72.3 1.9 convolution_add_fusion
  74.7 1.0 copy.28
  75.8 5.5 fusion.9
  81.3 1.0 copy.26
  82.6 3.8 convolution_convert_fusion.1
  86.4 4.7 copy.24
  91.1 40.3 %reduce-scatter.14.cloned.1.call-done = bf16[96,4]{1,0:T(8,128)(2,1)} async-done(((bf16[1536,4]{1,0:T(8,128)(2,1)}), bf16[96,4]{1,0:T(8,128)(2,1)}) %reduce-scatter.14.cloned.1.call-update) | async-done | bytes 784
  132.8 59.8 %reduce-scatter.12.cloned.1.call-done = bf16[96,4]{1,0:T(8,128)(2,1)} async-done(((bf16[1536,4]{1,0:T(8,128)(2,1)}), bf16[96,4]{1,0:T(8,128)(2,1)}) %reduce-scatter.12.cloned.1.call-update) | async-done | bytes 784
  194.0 155.6 %all-reduce.2.cloned.1.call-done = bf16[1536,32]{0,1:T(8,128)(2,1)} async-done(((bf16[1536,32]{0,1:T(8,128)(2,1)}), bf16[1536,32]{0,1:T(8,128)(2,1)}) %all-reduce.2.cloned.1.call-update) | async-done | bytes 98320 | tf_op jit(solution)/shard_map/psum | solution.py:76
  349.7 0.9 convert_element_type.90
  350.6 63.6 %while.13 = (s32[]{:T(128)}, f32[1536,32]{0,1:T(8,128)S(1)}, f32[1536,32]{0,1:T(8,128)S(1)}, s32[]{:T(128)}, f32[]{:T(128)}, /*index=5*/s32[]{:T(128)}) while((s32[]{:T(128)}, f32[1536,32]{0,1:T(8,128)S(1)}, f32[1536,32]{0,1:T(8,128)S(1)}, s32[]{:T(128)}, f32[]{:T(128)}, /*index=5*/s32[]{:T(128)}) %tuple.40), condition=%wide.region_7.8_spmd, body=%wide.region_5.7_spmd.sunk | while | flops 1185794 | bytes 436597 | solution.py:24
  350.8 0.9 multiply_reduce_fusion.3
  352.8 0.9 multiply_reduce_fusion.3
  358.8 0.9 multiply_reduce_fusion.3
  360.7 0.9 multiply_reduce_fusion.3
  362.7 0.9 multiply_reduce_fusion.3
  364.7 0.9 multiply_reduce_fusion.3
  366.7 0.9 multiply_reduce_fusion.3
  376.6 0.9 multiply_reduce_fusion.3
  380.6 0.9 multiply_reduce_fusion.3
  382.6 0.9 multiply_reduce_fusion.3
  414.2 3.1 convolution_convert_fusion.3
  417.2 140.4 %psum.15 = bf16[32,384]{1,0:T(8,128)(2,1)S(1)} all-reduce(bf16[32,384]{1,0:T(8,128)(2,1)S(1)} %convolution_convert_fusion.3), channel_id=1, replica_groups=mesh['dp'=32,'tensor'=16] {'dp'}, use_global_device_ids=true, to_apply=%region_8.9 | all-reduce | flops 12288 | bytes 49152 | tf_op jit(solution)/shard_map/psum | solution.py:81
  557.7 4.5 fusion.8
  562.1 1.1 copy.25
  563.2 1.4 multiply_convert_fusion
  (156 shorter events, 37.6 us)
Async XLA Ops:
  7.2 61.0 %copy-start = (bf16[1536,384]{1,0:T(8,128)(2,1)S(1)}, bf16[1536,384]{1,0:T(8,128)(2,1)}, u32[]{:S(2)}) copy-start(bf16[1536,384]{1,0:T(8,128)(2,1)} %param.12) | copy-start | bytes 3538948
  7.2 50.7 %all-gather.2.cloned.1.call-start = ((), (), s32[]{:S(2)}) async-start(), calls=%async_computation.3 | async-start | bytes 3342336 | tf_op jit(solution)/shard_map/all_gather | solution.py:37
  7.9 123.5 %reduce-scatter.14.cloned.1.call-start = ((), (), s32[]{:S(2)}) async-start(), calls=%async_computation.7 | async-start | bytes 417792
  14.1 48.4 %copy-start.5 = (f32[4,1536]{1,0:T(4,128)S(1)}, f32[4,1536]{1,0:T(4,128)}, u32[]{:S(2)}) copy-start(f32[4,1536]{1,0:T(4,128)} %param.17) | copy-start | bytes 73732
  62.5 5.7 copy-start.7
  70.5 1.9 copy-start.6
  72.3 1.9 copy-start.2
  74.2 8.3 %copy-start.3 = (f32[1536,384]{1,0:T(8,128)}, f32[1536,384]{1,0:T(8,128)S(1)}, u32[]{:S(2)}) copy-start(f32[1536,384]{1,0:T(8,128)S(1)} %convolution_add_fusion) | copy-start | bytes 7077892
  75.8 116.9 %reduce-scatter.12.cloned.1.call-start = ((), (), s32[]{:S(2)}) async-start(), calls=%async_computation.6 | async-start | bytes 417792
  82.3 267.3 %all-reduce.2.cloned.1.call-start = ((), (), s32[]{:S(2)}) async-start(), calls=%async_computation.4 | async-start | bytes 196608 | tf_op jit(solution)/shard_map/psum | solution.py:76
  86.3 475.8 %reduce-scatter.10.cloned.1.call-start = ((), (), s32[]{:S(2)}) async-start(), calls=%async_computation.5 | async-start | bytes 3342336
  414.2 148.0 %copy-start.1 = (f32[1536,32]{0,1:T(8,128)}, f32[1536,32]{0,1:T(8,128)S(1)}, u32[]{:S(2)}) copy-start(f32[1536,32]{0,1:T(8,128)S(1)} %get-tuple-element.70) | copy-start | bytes 589828
  557.7 7.0 %copy-start.4 = (f32[32,384]{1,0:T(8,128)}, f32[32,384]{1,0:T(8,128)S(1)}, u32[]{:S(2)}) copy-start(f32[32,384]{1,0:T(8,128)S(1)} %convert_multiply_fusion.5) | copy-start | bytes 147460
Sparse Core Ops, SparseCore 0:
  10.1 47.6 all-gather.1
  75.9 55.4 reduce-scatter.13
  135.0 57.5 reduce-scatter.11
  196.5 153.1 all-reduce.1
  352.3 59.1 reduce-scatter.9
where the time goes:
time: 573 us; the launch traced here: 572 us
  waiting for transfers between devices  300 us (52%)
  blocking collectives  140 us (24%)
  matrix products  69.2 us (12%)
  loops' own time  23.2 us (4%)
  local copies, waits for them, and re-layouts  19.9 us (3%)
  between operations  14 us (2%)
    psum x1, waiting for transfers between devices, local(): p_total = lax.psum(p_local.astype(jnp.bfloat16), 'dp').astype(jnp.float32)  156 us
    psum x1, blocking collectives, local(): lax.psum(q_local.astype(jnp.bfloat16), 'dp').astype(jnp.float32)  140 us
    unnamed x8, waiting for transfers between devices  101 us
    all_gather x1, waiting for transfers between devices, local(): rows = lax.all_gather(normed, 'tensor', axis=1, tiled=True)  43.8 us
    dot_general x32, matrix products, one_column(): column = column - jnp.dot(basis, coeffs, precision=lax.Precision.HIGHEST)  28.1 us
    another operation x1, loops' own time, orthonormal(): return lax.fori_loop(0, pmat.shape[1], one_column, jnp.zeros_like(pmat))  23.2 us
  transfers between devices with their start and end apart: 5, of which 4 were waited for; matrix products, arithmetic and copies ran while one was open for 13% of the time, Pallas kernels for 0%

commit v1 on v0

v1 whole, which is shorter than its diff:
```python
import functools

import jax
import jax.numpy as jnp
from jax import lax
from jax.experimental import pallas as pl
from jax.experimental.pallas import tpu as pltpu
from jax.sharding import Mesh, PartitionSpec as P

SEQ = 256
DP = ("x", "y")
TENSOR = ("z", "core")
BF = jnp.bfloat16
F32 = jnp.float32
NN = (((1,), (0,)), ((), ()))
NT = (((1,), (1,)), ((), ()))
TN = (((0,), (0,)), ((), ()))
MIB = 1024 * 1024


def mm(a, b, dims):
    return lax.dot_general(a, b, dims, preferred_element_type=F32)


def split(v):
    hi = v.astype(BF)
    return hi, (v - hi.astype(F32)).astype(BF)


def gelu_slope(u):
    cdf = 0.5 * (1.0 + lax.erf(u * 0.7071067811865476))
    dens = jnp.exp(-0.5 * u * u) * 0.3989422804014327
    return cdf + u * dens


def backward_kernel(lengths, rows, w_t, weight, cot_t, film, error, q_init,
                    part, moment, p_out, film_t, z_buf):
    s = pl.program_id(0)
    samples = pl.num_programs(0)

    @pl.when(s == 0)
    def _():
        film_t[...] = film[...].T

    for k in range(4):
        @pl.when(s == k)
        def _(k=k):
            scale = film_t[:, k:k + 1]
            shift = film_t[:, 4 + k:5 + k]
            z_buf[...] = (rows[...].astype(F32) * scale + shift).astype(BF)

    z = z_buf[...]
    u = mm(w_t[...], z, NN)
    position = lax.broadcasted_iota(jnp.int32, (1, SEQ), 1)
    valid = (position < lengths[s]).astype(F32)
    d_pre = (cot_t[...].astype(F32) * gelu_slope(u) * valid).astype(BF)
    part[...] = mm(weight[...], d_pre, NN).astype(BF)
    product = mm(z, d_pre, NT)

    @pl.when(s == 0)
    def _():
        moment[...] = product + error[0].astype(F32)

    @pl.when(s > 0)
    def _():
        moment[...] += product

    @pl.when(s == samples - 1)
    def _():
        m_hi, m_lo = split(moment[...])
        q_hi, q_lo = split(q_init[...])
        rank = q_init.shape[0]
        first = mm(jnp.concatenate([q_hi, q_lo], axis=0), m_hi, NT)
        p = first[:rank] + first[rank:] + mm(q_hi, m_lo, NT)
        for k in range(rank):
            p_out[k] = p[k:k + 1]


def backward(lengths, rows, w_t, weight, cot_t, film, error, q_init):
    width, tokens = rows.shape
    hidden = weight.shape[1]
    rank = q_init.shape[0]
    whole = lambda *shape: pl.BlockSpec(shape, lambda s: (0,) * len(shape))
    return pl.pallas_call(
        backward_kernel,
        grid=(tokens // SEQ,),
        in_specs=[
            pl.BlockSpec(memory_space=pltpu.SMEM),
            pl.BlockSpec((width, SEQ), lambda s: (0, s)),
            whole(hidden, width),
            whole(width, hidden),
            pl.BlockSpec((hidden, SEQ), lambda s: (0, s)),
            whole(8, width),
            whole(1, width, hidden),
            whole(rank, hidden),
        ],
        out_specs=[
            pl.BlockSpec((width, SEQ), lambda s: (0, s)),
            whole(width, hidden),
            whole(rank, 1, width),
        ],
        out_shape=[
            jax.ShapeDtypeStruct((width, tokens), BF),
            jax.ShapeDtypeStruct((width, hidden), F32),
            jax.ShapeDtypeStruct((rank, 1, width), F32),
        ],
        scratch_shapes=[pltpu.VMEM((width, 8), F32), pltpu.VMEM((width, SEQ), BF)],
        compiler_params=pltpu.CompilerParams(vmem_limit_bytes=48 * MIB),
        cost_estimate=pl.CostEstimate(
            flops=6 * tokens * width * hidden, bytes_accessed=14 * MIB, transcendentals=0
        ),
    )(lengths, rows, w_t, weight, cot_t, film, error, q_init)


def right_kernel(p_rows, moment, y_out):
    rank = p_rows.shape[0]
    p = jnp.concatenate([p_rows[k] for k in range(rank)], axis=0)
    p_hi, p_lo = split(p)
    m_hi, m_lo = split(moment[...])
    first = mm(jnp.concatenate([p_hi, p_lo], axis=0), m_hi, NN)
    y_out[...] = (first[:rank] + first[rank:] + mm(p_hi, m_lo, NN)).astype(BF)


def right_factor(p_rows, moment):
    rank = p_rows.shape[0]
    width, hidden = moment.shape
    return pl.pallas_call(
        right_kernel,
        out_shape=jax.ShapeDtypeStruct((rank, hidden), BF),
        compiler_params=pltpu.CompilerParams(vmem_limit_bytes=32 * MIB),
        cost_estimate=pl.CostEstimate(
            flops=6 * rank * width * hidden, bytes_accessed=3 * MIB, transcendentals=0
        ),
    )(p_rows, moment)


def gram_schmidt_kernel(p_rows, basis_out, mix_out, p, work):
    rank, _, width = p_rows.shape
    for k in range(rank):
        p[pl.ds(k, 1), :] = p_rows[k]
        work[pl.ds(k, 1), :width] = p_rows[k]
    row_id = lax.broadcasted_iota(jnp.int32, (rank, 1), 0)
    eye_row = lax.broadcasted_iota(jnp.int32, (rank, 128), 0)
    eye_col = lax.broadcasted_iota(jnp.int32, (rank, 128), 1)
    work[:, width:] = (eye_row == eye_col).astype(F32)

    def step(i, carry):
        row = work[pl.ds(i, 1), :]
        main = row[:, :width]
        norm = jnp.sqrt(jnp.sum(main * main, axis=1, keepdims=True))
        unit = row / (norm + 1e-06)
        coeffs = jnp.sum(p[...] * unit[:, :width], axis=1, keepdims=True)
        coeffs = jnp.where(row_id > i, coeffs, 0.0)
        work[...] = jnp.where(row_id == i, unit, work[...] - coeffs * unit)
        return carry

    lax.fori_loop(0, rank, step, 0)
    basis_out[...] = work[:, :width]
    mix_out[...] = work[:, width:]


def gram_schmidt(p_rows):
    rank, _, width = p_rows.shape
    return pl.pallas_call(
        gram_schmidt_kernel,
        out_shape=[
            jax.ShapeDtypeStruct((rank, width), F32),
            jax.ShapeDtypeStruct((rank, 128), F32),
        ],
        scratch_shapes=[pltpu.VMEM((rank, width), F32), pltpu.VMEM((rank, width + 128), F32)],
        compiler_params=pltpu.CompilerParams(vmem_limit_bytes=16 * MIB),
        cost_estimate=pl.CostEstimate(
            flops=4 * rank * rank * width, bytes_accessed=MIB, transcendentals=0
        ),
    )(p_rows)


def finish_kernel(replicas, y_parts, mix, basis, moment, q_out, error_out, q_buf):
    rank = q_out.shape[0]

    @pl.when(pl.program_id(0) == 0)
    def _():
        y = y_parts[0].astype(F32)
        for k in range(1, y_parts.shape[0]):
            y = y + y_parts[k].astype(F32)
        y_hi, y_lo = split(y * (1.0 / replicas))
        a_hi, a_lo = split(mix[:, :rank])
        q_new = mm(a_hi, y_hi, NN) + mm(a_lo, y_hi, NN) + mm(a_hi, y_lo, NN)
        q_out[...] = q_new
        q_hi, q_lo = split(q_new)
        q_buf[...] = jnp.concatenate([q_hi, q_hi, q_lo], axis=0)

    b_hi, b_lo = split(basis[...])
    averaged = mm(jnp.concatenate([b_hi, b_lo, b_hi], axis=0), q_buf[...], TN)
    error_out[0] = (moment[...] - averaged).astype(BF)


def finish(replicas, y_parts, mix, basis, moment):
    width, hidden = moment.shape
    rank = basis.shape[0]
    block = width // 4
    return pl.pallas_call(
        functools.partial(finish_kernel, replicas),
        grid=(4,),
        in_specs=[
            pl.BlockSpec(y_parts.shape, lambda i: (0, 0, 0)),
            pl.BlockSpec(mix.shape, lambda i: (0, 0)),
            pl.BlockSpec((rank, block), lambda i: (0, i)),
            pl.BlockSpec((block, hidden), lambda i: (i, 0)),
        ],
        out_specs=[
            pl.BlockSpec((rank, hidden), lambda i: (0, 0)),
            pl.BlockSpec((1, block, hidden), lambda i: (0, i, 0)),
        ],
        out_shape=[
            jax.ShapeDtypeStruct((rank, hidden), F32),
            jax.ShapeDtypeStruct((1, width, hidden), BF),
        ],
        scratch_shapes=[pltpu.VMEM((3 * rank, hidden), BF)],
        compiler_params=pltpu.CompilerParams(vmem_limit_bytes=16 * MIB),
        cost_estimate=pl.CostEstimate(
            flops=6 * rank * width * hidden, bytes_accessed=4 * MIB, transcendentals=0
        ),
    )(y_parts, mix, basis, moment)


def film_kernel(dz_t, rows, scale_t, d_normed, d_scale, d_shift):
    width, tokens = dz_t.shape
    samples = scale_t.shape[1]
    dz = dz_t[...]
    wide = dz.astype(F32)
    for k in range(samples):
        cut = slice(k * SEQ, (k + 1) * SEQ)
        d_normed[:, cut] = (wide[:, cut] * scale_t[:, k:k + 1]).astype(BF)
    sample = lax.broadcasted_iota(jnp.int32, (8, tokens), 0)
    token = lax.broadcasted_iota(jnp.int32, (8, tokens), 1)
    table = (token // SEQ == sample).astype(BF)
    hi, lo = split(wide * rows[...].astype(F32))
    d_scale[...] = (mm(table, hi, NT) + mm(table, lo, NT))[:samples]
    d_shift[...] = mm(table, dz, NT)[:samples]


def film_gradients(dz_t, rows, scale_t):
    width, tokens = dz_t.shape
    samples = scale_t.shape[1]
    return pl.pallas_call(
        film_kernel,
        out_shape=[
            jax.ShapeDtypeStruct((width, tokens), BF),
            jax.ShapeDtypeStruct((samples, width), F32),
            jax.ShapeDtypeStruct((samples, width), F32),
        ],
        compiler_params=pltpu.CompilerParams(vmem_limit_bytes=16 * MIB),
        cost_estimate=pl.CostEstimate(
            flops=64 * tokens * width, bytes_accessed=MIB, transcendentals=0
        ),
    )(dz_t, rows, scale_t)


def local(normed, cotangent, weight, error, q_init, lengths, film_scale, film_shift):
    replicas = lax.axis_size(DP)
    col_width = normed.shape[1]
    rank, hidden = q_init.shape
    own = normed.T
    rows = lax.all_gather(own, TENSOR, axis=0, tiled=True)
    film = jnp.concatenate([film_scale, film_shift], axis=0)
    part, moment, p_local = backward(
        lengths, rows, weight.T, weight, cotangent.T, film, error, q_init
    )

    dz = lax.psum_scatter(part, TENSOR, scatter_dimension=0, tiled=True)
    start = lax.axis_index(TENSOR) * col_width
    own_scale = lax.dynamic_slice_in_dim(film_scale, start, col_width, 1).T
    d_normed, d_scale, d_shift = film_gradients(dz, own, own_scale)

    p_parts = lax.all_to_all(p_local, DP, 0, 0, tiled=True)
    p_row = jnp.sum(p_parts, axis=0)
    p_rows = lax.all_to_all(
        jnp.broadcast_to(p_row[None], (replicas,) + p_row.shape), DP, 0, 0, tiled=True
    )
    y = right_factor(p_rows, moment)
    basis, mix = gram_schmidt(p_rows)
    nx, ny = lax.axis_size("x"), lax.axis_size("y")
    y_x = lax.all_to_all(jnp.broadcast_to(y[None], (nx, rank, hidden)), "x", 0, 0, tiled=True)
    y = jnp.sum(y_x.astype(F32), axis=0).astype(BF)
    y_y = lax.all_to_all(jnp.broadcast_to(y[None], (ny, rank, hidden)), "y", 0, 0, tiled=True)
    q_new, new_error = finish(replicas, y_y, mix, basis, moment)
    return (d_normed.T, d_scale, d_shift, basis[None], q_new, new_error)


def solution(mesh):
    x, y, z = 4, 8, 8
    grid = Mesh(mesh.devices.reshape(x, y, z, 2), ("x", "y", "z", "core"))
    return jax.shard_map(
        local,
        mesh=grid,
        in_specs=(
            P(DP, TENSOR),
            P(DP, TENSOR),
            P(None, TENSOR),
            P(DP, None, TENSOR),
            P(None, TENSOR),
            P(DP),
            P(DP, None),
            P(DP, None),
        ),
        out_specs=(
            P(DP, TENSOR),
            P(DP, TENSOR),
            P(DP, TENSOR),
            P(TENSOR, None, None),
            P(None, TENSOR),
            P(DP, None, TENSOR),
        ),
        check_vma=False,
    )
```

time: 573 us -> 148 us (0.26)
  the two profiles are of different devices: /device:TPU:64 before, /device:TPU:1 now
where the time goes in v1:
time: 148 us; the launch traced here: 146 us
  waiting for transfers between devices  53.5 us (36%)
  blocking collectives  40.3 us (27%)
  Pallas kernels  27 us (18%)
  between operations  14.2 us (10%)
  local copies, waits for them, and re-layouts  7.22 us (5%)
  starting transfers between devices  3.47 us (2%)
    all_gather x1, waiting for transfers between devices, local(): rows = lax.all_gather(own, TENSOR, axis=0, tiled=True)  49.4 us
    all_to_all x1, blocking collectives, local(): p_parts = lax.all_to_all(p_local, DP, 0, 0, tiled=True)  18.6 us
    pallas_call x1, Pallas kernels, backward(): pl.pallas_call(backward_kernel, grid=(tokens // SEQ,), in_specs=[pl.Block...  15.1 us
    all_to_all x1, blocking collectives, local(): lax.all_to_all(jnp.broadcast_to(p_row[None], (replicas,) + p_row.shape),...  14.7 us
    pallas_call x1, Pallas kernels, gram_schmidt(): pl.pallas_call(gram_schmidt_kernel, out_shape=[jax.ShapeDtypeStruct((rank...  7.9 us
    all_to_all x1, blocking collectives, local(): lax.all_to_all(jnp.broadcast_to(y[None], (nx, rank, hidden)), 'x', 0, 0,...  7.03 us
    unnamed x23, local copies, waits for them, and re-layouts  6.33 us
    all_to_all x1, starting transfers between devices, local(): lax.all_to_all(jnp.broadcast_to(y[None], (ny, rank, hidden)), 'y', 0, 0,...  3.39 us
  transfers between devices with their start and end apart: 3, of which 3 were waited for; matrix products, arithmetic and copies ran while one was open for 3% of the time, Pallas kernels for 7%

profile of v1, /device:TPU:1, one launch (start us, length us, event | category | flops | bytes accessed | tf_op | source)
XLA Modules:
  0.0 145.7 jit_solution(15175780499416903066)
XLA Ops:
  7.2 0.0 all-gather.2.cloned.1.call-start
  7.2 0.7 all-gather.2.cloned.1.call-update
  7.9 0.0 reduce-scatter.2.cloned.1.call-start
  7.9 1.6 %copy.17 = bf16[1536,384]{0,1:T(8,128)(2,1)S(1)} copy(bf16[1536,384]{1,0:T(8,128)(2,1)} %weight.1) | data formatting | bytes 2359296 | tf_op args[2]
  9.5 0.0 copy-start.8
  9.5 0.0 copy-start.9
  9.5 0.0 copy-start.1
  9.6 0.0 copy-start.6
  9.6 0.0 copy-start.7
  9.6 1.5 %copy.18 = bf16[1024,384]{0,1:T(8,128)(2,1)S(1)} copy(bf16[1024,384]{1,0:T(8,128)(2,1)} %param.9) | data formatting | bytes 1572864 | tf_op args[1]
  11.1 49.4 %all-gather.2.cloned.1.call-done.rows = bf16[1536,1024]{1,0:T(8,128)(2,1)} async-done(((bf16[96,1024]{1,0:T(8,128)(2,1)}), bf16[1536,1024]{1,0:T(8,128)(2,1)}) %all-gather.2.cloned.1.call-update) | async-done | bytes 3145744 | tf_op jit(solution)/shard_map/all_gather | solution.py:265
  60.5 0.0 copy-done.6
  60.6 1.3 copy-done.5
  61.8 15.1 %shard_map.127 = (bf16[1536,1024]{1,0:T(8,128)(2,1)}, f32[1536,384]{1,0:T(8,128)}, f32[32,1,1536]{2,1,0:T(1,128)S(1)}) custom-call(s32[4]{0:T(128)S(1)} %copy-done.7, bf16[1536,1024]{1,0:T(8,128)(2,1)} %all-gather.2.cloned.1.call-done.rows, bf16[384,1536]{1,0:T(8,128)(2,1)S(1)} %bitcast.6, bf16[1536,384]{1,0:T(8,128)(2,1)S(1)} %copy-done.1, ...), custom_call_target="tpu_custom_call" | custom-call | flops 3623878656 | bytes 14680064 | tf_op jit(solution)/shard_map/pallas_call | solution.py:84
  77.0 0.0 reduce-scatter.2.cloned.1.call-update
  77.0 18.6 %all_to_all.20 = f32[32,1,1536]{2,1,0:T(1,128)S(1)} all-to-all(f32[32,1,1536]{2,1,0:T(1,128)S(1)} %get-tuple-element.20), channel_id=1, replica_groups=mesh['x'=4,'y'=8,'z'=8,'core'=2] {'x','y'}, dimensions={0} | all-to-all | bytes 393216 | tf_op jit(solution)/shard_map/all_to_all | solution.py:276
  95.6 0.1 reduce_sum.21
  95.7 0.1 broadcast_in_dim.8
  95.8 14.7 %all_to_all.21.p_rows = f32[32,1,1536]{2,1,0:T(1,128)S(1)} all-to-all(f32[32,1,1536]{2,1,0:T(1,128)S(1)} %broadcast_in_dim.8), channel_id=1, replica_groups=mesh['x'=4,'y'=8,'z'=8,'core'=2] {'x','y'}, dimensions={0} | all-to-all | bytes 393216 | tf_op jit(solution)/shard_map/all_to_all | solution.py:278
  110.5 0.6 shard_map.130
  111.1 7.0 %all_to_all.22 = bf16[4,32,384]{2,1,0:T(8,128)(2,1)S(1)} all-to-all(bf16[4,32,384]{2,1,0:T(8,128)(2,1)S(1)} %broadcast_in_dim.10), channel_id=1, replica_groups=mesh['x'=4,'y'=8,'z'=8,'core'=2] {'x'}, dimensions={0} | all-to-all | bytes 196608 | tf_op jit(solution)/shard_map/all_to_all | solution.py:284
  118.1 0.7 broadcast_in_dim.11
  118.8 3.4 %all-to-all-start.3 = ((bf16[8,32,384]{2,1,0:T(8,128)(2,1)}), bf16[8,32,384]{2,1,0:T(8,128)(2,1)S(1)}, u32[]{:S(2)}, u32[]{:S(2)}) async-start(bf16[8,32,384]{2,1,0:T(8,128)(2,1)} %broadcast_in_dim.11), calls=%async_computation.4 | async-start | bytes 393216 | tf_op jit(solution)/shard_map/all_to_all | solution.py:286
  122.2 0.1 constant_dynamic-slice_fusion
  122.3 0.1 copy.20
  122.4 7.9 %shard_map.129 = (f32[32,1536]{1,0:T(8,128)}, f32[32,128]{1,0:T(8,128)S(1)}) custom-call(f32[32,1,1536]{2,1,0:T(1,128)S(1)} %all_to_all.21.p_rows), custom_call_target="tpu_custom_call" | custom-call | flops 6291456 | bytes 1048576 | tf_op jit(solution)/shard_map/pallas_call | solution.py:164
  130.3 0.4 all-to-all-done.3.y_parts
  130.8 0.9 copy-done.4
  131.7 2.4 %shard_map.131 = (f32[32,384]{1,0:T(8,128)}, bf16[1,1536,384]{2,1,0:T(8,128)(2,1)}) custom-call(bf16[8,32,384]{2,1,0:T(8,128)(2,1)S(1)} %all-to-all-done.3.y_parts, f32[32,128]{1,0:T(8,128)S(1)} %get-tuple-element.23.mix, f32[32,1536]{1,0:T(8,128)S(1)} %copy-done.4, f32[1536,384]{1,0:T(8,128)S(1)} %copy-done), custom_call_target="tpu_custom_call" | custom-call | flops 113246208 | bytes 4194304 | tf_op jit(solution)/shard_map/pallas_call | solution.py:202
  134.1 2.9 %reduce-scatter.2.cloned.1.call-done.dz_t = bf16[96,1024]{1,0:T(8,128)(2,1)} async-done(((bf16[1536,1024]{1,0:T(8,128)(2,1)}), bf16[96,1024]{1,0:T(8,128)(2,1)}) %reduce-scatter.2.cloned.1.call-update) | async-done | bytes 196624 | tf_op jit(solution)/shard_map/reduce_scatter | solution.py:271
  137.1 0.9 copy-done.3
  138.0 0.9 shard_map.128
  (14 shorter events, 0.1 us)
Async XLA Ops:
  7.2 53.4 %all-gather.2.cloned.1.call-start = ((), (), s32[]{:S(2)}) async-start(), calls=%async_computation.5 | async-start | bytes 3342336 | tf_op jit(solution)/shard_map/all_gather | solution.py:265
  7.9 129.2 %reduce-scatter.2.cloned.1.call-start = ((), (), s32[]{:S(2)}) async-start(), calls=%async_computation.6 | async-start | bytes 3342336 | tf_op jit(solution)/shard_map/reduce_scatter | solution.py:271
  9.5 1.6 %copy-start.8 = (f32[4,1536]{1,0:T(4,128)S(1)}, f32[4,1536]{1,0:T(4,128)}, u32[]{:S(2)}) copy-start(f32[4,1536]{1,0:T(4,128)} %param.14) | copy-start | bytes 73732
  9.5 1.6 %copy-start.9 = (f32[4,1536]{1,0:T(4,128)S(1)}, f32[4,1536]{1,0:T(4,128)}, u32[]{:S(2)}) copy-start(f32[4,1536]{1,0:T(4,128)} %param.15) | copy-start | bytes 73732
  9.5 51.0 %copy-start.1 = (bf16[1536,384]{1,0:T(8,128)(2,1)S(1)}, bf16[1536,384]{1,0:T(8,128)(2,1)}, u32[]{:S(2)}) copy-start(bf16[1536,384]{1,0:T(8,128)(2,1)} %weight.1) | copy-start | bytes 3538948
  9.6 51.0 %copy-start.6 = (f32[32,384]{1,0:T(8,128)S(1)}, f32[32,384]{1,0:T(8,128)}, u32[]{:S(2)}) copy-start(f32[32,384]{1,0:T(8,128)} %q_init.1) | copy-start | bytes 147460
  9.6 51.0 %copy-start.7 = (s32[4]{0:T(128)S(1)}, s32[4]{0:T(128)}, u32[]{:S(2)}) copy-start(s32[4]{0:T(128)} %lengths.1) | copy-start | bytes 52
  60.6 1.3 copy-start.5
  77.0 33.5 %copy-start = (f32[1536,384]{1,0:T(8,128)S(1)}, f32[1536,384]{1,0:T(8,128)}, u32[]{:S(2)}) copy-start(f32[1536,384]{1,0:T(8,128)} %get-tuple-element.22.moment) | copy-start | bytes 7077892
  118.8 11.9 %all-to-all-start.3 = ((bf16[8,32,384]{2,1,0:T(8,128)(2,1)}), bf16[8,32,384]{2,1,0:T(8,128)(2,1)S(1)}, u32[]{:S(2)}, u32[]{:S(2)}) async-start(bf16[8,32,384]{2,1,0:T(8,128)(2,1)} %broadcast_in_dim.11), calls=%async_computation.4 | async-start | bytes 393216 | tf_op jit(solution)/shard_map/all_to_all | solution.py:286
  130.8 0.9 copy-start.4
  131.7 5.4 %copy-start.2 = (bf16[1024,96]{0,1:T(8,128)(2,1)S(1)}, bf16[1024,96]{0,1:T(8,128)(2,1)}, u32[]{:S(2)}) copy-start(bf16[1024,96]{0,1:T(8,128)(2,1)} %param.8) | copy-start | bytes 589828
  137.1 0.9 copy-start.3
Sparse Core Ops, SparseCore 0:
  10.1 50.3 all-gather.1
  77.1 59.9 reduce-scatter.1

commit v2 on v1

v2 whole, which is shorter than its diff:
```python
import functools

import jax
import jax.numpy as jnp
from jax import lax
from jax.experimental import pallas as pl
from jax.experimental.pallas import tpu as pltpu
from jax.sharding import Mesh, PartitionSpec as P

SEQ = 256
DP = ("x", "y")
TENSOR = ("z", "core")
SWAP = [(0, 1), (1, 0)]
BF = jnp.bfloat16
F32 = jnp.float32
NN = (((1,), (0,)), ((), ()))
NT = (((1,), (1,)), ((), ()))
TN = (((0,), (0,)), ((), ()))
MIB = 1024 * 1024
CHUNKS = 3
IN_VMEM = pl.BlockSpec(memory_space=pltpu.VMEM)
IN_HBM = pl.BlockSpec(memory_space=pltpu.HBM)


def mm(a, b, dims):
    return lax.dot_general(a, b, dims, preferred_element_type=F32)


def split(v):
    hi = v.astype(BF)
    return hi, (v - hi.astype(F32)).astype(BF)


def gelu_slope(u):
    cdf = 0.5 * (1.0 + lax.erf(u * 0.7071067811865476))
    dens = jnp.exp(-0.5 * u * u) * 0.3989422804014327
    return cdf + u * dens


def backward_kernel(lengths, rows, w_t, weight, cot_t, film, error, q_init,
                    part, moment, p_out,
                    row_buf, wt_buf, w_buf, cot_buf, err_buf, z_buf, part_buf, m_buf, sems):
    width = rows.shape[0]
    rank = q_init.shape[0]
    samples = lengths.shape[0]
    step = width // CHUNKS
    cuts = [pl.ds(c * step, step) for c in range(CHUNKS)]
    sem = iter(range(sems.shape[0]))

    def fetch(source, target):
        copy = pltpu.make_async_copy(source, target, sems.at[next(sem)])
        copy.start()
        return copy

    get_rows = [fetch(rows.at[cuts[0]], row_buf.at[cuts[0]])]
    get_wt = fetch(w_t, wt_buf)
    get_rows += [fetch(rows.at[cut], row_buf.at[cut]) for cut in cuts[1:]]
    get_cot = fetch(cot_t, cot_buf)
    get_w = fetch(weight, w_buf)
    get_error = fetch(error.at[0], err_buf)

    film_t = film[...].T
    u = None
    for c in range(CHUNKS):
        cut = slice(c * step, (c + 1) * step)
        get_rows[c].wait()
        z = jnp.concatenate(
            [
                (
                    row_buf[cut, k * SEQ:(k + 1) * SEQ].astype(F32) * film_t[cut, k:k + 1]
                    + film_t[cut, samples + k:samples + k + 1]
                ).astype(BF)
                for k in range(samples)
            ],
            axis=1,
        )
        z_buf[cut, :] = z
        if c == 0:
            get_wt.wait()
        term = mm(wt_buf[:, cut], z, NN)
        u = term if u is None else u + term
    position = lax.broadcasted_iota(jnp.int32, (1, SEQ), 1)
    valid = jnp.concatenate(
        [(position < lengths[k]).astype(F32) for k in range(samples)], axis=1
    )
    get_cot.wait()
    d_pre = (cot_buf[...].astype(F32) * gelu_slope(u) * valid).astype(BF)
    get_w.wait()
    puts = []
    for c in range(CHUNKS):
        cut = slice(c * step, (c + 1) * step)
        part_buf[cut, :] = mm(w_buf[cut, :], d_pre, NN).astype(BF)
        puts.append(fetch(part_buf.at[cuts[c]], part.at[cuts[c]]))
    get_error.wait()
    q_hi, q_lo = split(q_init[...])
    q_both = jnp.concatenate([q_hi, q_lo], axis=0)
    for c in range(CHUNKS):
        cut = slice(c * step, (c + 1) * step)
        total = mm(z_buf[cut, :], d_pre, NT) + err_buf[cut, :].astype(F32)
        m_buf[cut, :] = total
        puts.append(fetch(m_buf.at[cuts[c]], moment.at[cuts[c]]))
        m_hi, m_lo = split(total)
        first = mm(q_both, m_hi, NT)
        p = first[:rank] + first[rank:] + mm(q_hi, m_lo, NT)
        for k in range(rank):
            p_out[k, :, cut] = p[k:k + 1]
    for put in puts:
        put.wait()


def backward(lengths, rows, w_t, weight, cot_t, film, error, q_init):
    width, tokens = rows.shape
    rank, hidden = q_init.shape
    return pl.pallas_call(
        backward_kernel,
        in_specs=[pl.BlockSpec(memory_space=pltpu.SMEM)]
        + [IN_HBM] * 4 + [IN_VMEM, IN_HBM, IN_VMEM],
        out_specs=[IN_HBM, IN_HBM, IN_VMEM],
        out_shape=[
            jax.ShapeDtypeStruct((width, tokens), BF),
            jax.ShapeDtypeStruct((width, hidden), F32),
            jax.ShapeDtypeStruct((rank, 1, width), F32),
        ],
        scratch_shapes=[
            pltpu.VMEM((width, tokens), BF),
            pltpu.VMEM((hidden, width), BF),
            pltpu.VMEM((width, hidden), BF),
            pltpu.VMEM((hidden, tokens), BF),
            pltpu.VMEM((width, hidden), BF),
            pltpu.VMEM((width, tokens), BF),
            pltpu.VMEM((width, tokens), BF),
            pltpu.VMEM((width, hidden), F32),
            pltpu.SemaphoreType.DMA((3 * CHUNKS + 4,)),
        ],
        compiler_params=pltpu.CompilerParams(vmem_limit_bytes=58 * MIB),
        cost_estimate=pl.CostEstimate(
            flops=6 * tokens * width * hidden, bytes_accessed=14 * MIB, transcendentals=0
        ),
    )(lengths, rows, w_t, weight, cot_t, film, error, q_init)


def right_kernel(p_rows, moment, y_out):
    rank = p_rows.shape[0]
    p = jnp.concatenate([p_rows[k] for k in range(rank)], axis=0)
    p_hi, p_lo = split(p)
    m_hi, m_lo = split(moment[...])
    first = mm(jnp.concatenate([p_hi, p_lo], axis=0), m_hi, NN)
    y_out[...] = (first[:rank] + first[rank:] + mm(p_hi, m_lo, NN)).astype(BF)


def right_factor(p_rows, moment):
    rank = p_rows.shape[0]
    width, hidden = moment.shape
    return pl.pallas_call(
        right_kernel,
        out_shape=jax.ShapeDtypeStruct((rank, hidden), BF),
        compiler_params=pltpu.CompilerParams(vmem_limit_bytes=32 * MIB),
        cost_estimate=pl.CostEstimate(
            flops=6 * rank * width * hidden, bytes_accessed=3 * MIB, transcendentals=0
        ),
    )(p_rows, moment)


def gram_schmidt_kernel(p_rows, basis_out, mix_out, stack_out, p, work):
    rank, _, width = p_rows.shape
    for k in range(rank):
        p[k:k + 1, :] = p_rows[k]
        work[k:k + 1, :width] = p_rows[k]
    eye_row = lax.broadcasted_iota(jnp.int32, (rank, 128), 0)
    eye_col = lax.broadcasted_iota(jnp.int32, (rank, 128), 1)
    work[:, width:] = (eye_row == eye_col).astype(F32)
    for i in range(rank):
        top = i // 8 * 8
        row_id = lax.broadcasted_iota(jnp.int32, (rank - top, 1), 0) + top
        row = work[i:i + 1, :]
        main = row[:, :width]
        square = jnp.sum(main * main, axis=1, keepdims=True)
        dots = jnp.sum(p[top:, :] * main, axis=1, keepdims=True)
        inverse = 1.0 / (jnp.sqrt(square) + 1e-06)
        unit = row * inverse
        coeffs = jnp.where(row_id > i, dots * inverse, 0.0)
        work[top:, :] = jnp.where(row_id == i, unit, work[top:, :] - coeffs * unit)
    basis = work[:, :width]
    basis_out[...] = basis
    mix_out[...] = work[:, width:]
    hi, lo = split(basis)
    stack_out[...] = jnp.concatenate([hi, lo, hi], axis=0)


def gram_schmidt(p_rows):
    rank, _, width = p_rows.shape
    return pl.pallas_call(
        gram_schmidt_kernel,
        out_shape=[
            jax.ShapeDtypeStruct((rank, width), F32),
            jax.ShapeDtypeStruct((rank, 128), F32),
            jax.ShapeDtypeStruct((3 * rank, width), BF),
        ],
        scratch_shapes=[pltpu.VMEM((rank, width), F32), pltpu.VMEM((rank, width + 128), F32)],
        compiler_params=pltpu.CompilerParams(vmem_limit_bytes=16 * MIB),
        cost_estimate=pl.CostEstimate(
            flops=4 * rank * rank * width, bytes_accessed=MIB, transcendentals=0
        ),
    )(p_rows)


def finish_kernel(replicas, y_parts, mix, stack, moment, q_out, error_out, q_buf):
    rank = q_out.shape[0]

    @pl.when(pl.program_id(0) == 0)
    def _():
        y = y_parts[0].astype(F32)
        for k in range(1, y_parts.shape[0]):
            y = y + y_parts[k].astype(F32)
        y_hi, y_lo = split(y * (1.0 / replicas))
        a_hi, a_lo = split(mix[:, :rank])
        q_new = mm(a_hi, y_hi, NN) + mm(a_lo, y_hi, NN) + mm(a_hi, y_lo, NN)
        q_out[...] = q_new
        q_hi, q_lo = split(q_new)
        q_buf[...] = jnp.concatenate([q_hi, q_hi, q_lo], axis=0)

    averaged = mm(stack[...], q_buf[...], TN)
    error_out[0] = (moment[...] - averaged).astype(BF)


def finish(replicas, y_parts, mix, stack, moment):
    width, hidden = moment.shape
    rank = mix.shape[0]
    block = width // 4
    return pl.pallas_call(
        functools.partial(finish_kernel, replicas),
        grid=(4,),
        in_specs=[
            pl.BlockSpec(y_parts.shape, lambda i: (0, 0, 0)),
            pl.BlockSpec(mix.shape, lambda i: (0, 0)),
            pl.BlockSpec((3 * rank, block), lambda i: (0, i)),
            pl.BlockSpec((block, hidden), lambda i: (i, 0)),
        ],
        out_specs=[
            pl.BlockSpec((rank, hidden), lambda i: (0, 0)),
            pl.BlockSpec((1, block, hidden), lambda i: (0, i, 0)),
        ],
        out_shape=[
            jax.ShapeDtypeStruct((rank, hidden), F32),
            jax.ShapeDtypeStruct((1, width, hidden), BF),
        ],
        scratch_shapes=[pltpu.VMEM((3 * rank, hidden), BF)],
        compiler_params=pltpu.CompilerParams(vmem_limit_bytes=16 * MIB),
        cost_estimate=pl.CostEstimate(
            flops=6 * rank * width * hidden, bytes_accessed=4 * MIB, transcendentals=0
        ),
    )(y_parts, mix, stack, moment)


def film_kernel(core, dz_own, dz_peer, rows, scale_t, d_normed, d_scale, d_shift):
    _, width, tokens = dz_own.shape
    samples = scale_t.shape[1]
    wide = dz_own[core[0]].astype(F32) + dz_peer[core[0]].astype(F32)
    for k in range(samples):
        cut = slice(k * SEQ, (k + 1) * SEQ)
        d_normed[:, cut] = (wide[:, cut] * scale_t[:, k:k + 1]).astype(BF)
    sample = lax.broadcasted_iota(jnp.int32, (8, tokens), 0)
    token = lax.broadcasted_iota(jnp.int32, (8, tokens), 1)
    table = (token // SEQ == sample).astype(BF)
    hi, lo = split(wide * rows[...].astype(F32))
    d_scale[...] = (mm(table, hi, NT) + mm(table, lo, NT))[:samples]
    hi, lo = split(wide)
    d_shift[...] = (mm(table, hi, NT) + mm(table, lo, NT))[:samples]


def film_gradients(core, dz_own, dz_peer, rows, scale_t):
    _, width, tokens = dz_own.shape
    samples = scale_t.shape[1]
    return pl.pallas_call(
        film_kernel,
        in_specs=[pl.BlockSpec(memory_space=pltpu.SMEM)] + [IN_VMEM] * 4,
        out_shape=[
            jax.ShapeDtypeStruct((width, tokens), BF),
            jax.ShapeDtypeStruct((samples, width), F32),
            jax.ShapeDtypeStruct((samples, width), F32),
        ],
        compiler_params=pltpu.CompilerParams(vmem_limit_bytes=16 * MIB),
        cost_estimate=pl.CostEstimate(
            flops=64 * tokens * width, bytes_accessed=MIB, transcendentals=0
        ),
    )(core, dz_own, dz_peer, rows, scale_t)


def local(normed, cotangent, weight, error, q_init, lengths, film_scale, film_shift):
    replicas = lax.axis_size(DP)
    col_width = normed.shape[1]
    rank, hidden = q_init.shape
    own = normed.T
    rows = lax.all_gather(own, TENSOR, axis=0, tiled=True)
    film = jnp.concatenate([film_scale, film_shift], axis=0)
    core = lax.axis_index("core")
    start = lax.axis_index(TENSOR) * col_width
    own_scale = lax.dynamic_slice_in_dim(film_scale, start, col_width, 1).T
    film, own_scale = lax.optimization_barrier((film, own_scale))
    part, moment, p_local = backward(
        lengths, rows, weight.T, weight, cotangent.T, film, error, q_init
    )

    dz_pair = lax.psum_scatter(part, "z", scatter_dimension=0, tiled=True)
    dz_pair = dz_pair.reshape(2, col_width, -1)
    dz_peer = lax.ppermute(dz_pair, "core", SWAP)
    d_normed, d_scale, d_shift = film_gradients(
        core.reshape(1), dz_pair, dz_peer, own, own_scale
    )

    p_parts = lax.all_to_all(p_local, DP, 0, 0, tiled=True)
    p_row = jnp.sum(p_parts, axis=0)
    p_rows = lax.all_to_all(
        jnp.broadcast_to(p_row[None], (replicas,) + p_row.shape), DP, 0, 0, tiled=True
    )
    y = right_factor(p_rows, moment)
    basis, mix, stack = gram_schmidt(p_rows)
    nx, ny = lax.axis_size("x"), lax.axis_size("y")
    y_x = lax.all_to_all(jnp.broadcast_to(y[None], (nx, rank, hidden)), "x", 0, 0, tiled=True)
    y = jnp.sum(y_x.astype(F32), axis=0).astype(BF)
    y_y = lax.all_to_all(jnp.broadcast_to(y[None], (ny, rank, hidden)), "y", 0, 0, tiled=True)
    q_new, new_error = finish(replicas, y_y, mix, stack, moment)
    return (d_normed.T, d_scale, d_shift, basis[None], q_new, new_error)


def solution(mesh):
    x, y, z = 4, 8, 8
    grid = Mesh(mesh.devices.reshape(x, y, z, 2), ("x", "y", "z", "core"))
    return jax.shard_map(
        local,
        mesh=grid,
        in_specs=(
            P(DP, TENSOR),
            P(DP, TENSOR),
            P(None, TENSOR),
            P(DP, None, TENSOR),
            P(None, TENSOR),
            P(DP),
            P(DP, None),
            P(DP, None),
        ),
        out_specs=(
            P(DP, TENSOR),
            P(DP, TENSOR),
            P(DP, TENSOR),
            P(TENSOR, None, None),
            P(None, TENSOR),
            P(DP, None, TENSOR),
        ),
        check_vma=False,
    )
```

time: 148 us -> 153 us (1.034)
  starting transfers between devices: 3.47 us -> 14.9 us
  blocking collectives: 40.3 us -> 33.1 us
  waiting for transfers between devices: 53.5 us -> 60.2 us
  Pallas kernels: 27 us -> 21.2 us
    all_to_all x1 -> x0, blocking collectives: 7.03 us -> none  [local(): lax.all_to_all(jnp.broadcast_to(y[None], (nx, rank, hidden)), 'x', 0, 0,...]
    all_to_all x1, waiting for transfers between devices: 0.45 us -> 6.17 us  [local(): lax.all_to_all(jnp.broadcast_to(y[None], (ny, rank, hidden)), 'y', 0, 0,...]
    ppermute x0 -> x1, starting transfers between devices: none -> 5.07 us  [local(): dz_peer = lax.ppermute(dz_pair, 'core', SWAP)]
    reduce_scatter x1, waiting for transfers between devices: 2.94 us -> 6.79 us  [local(): dz_pair = lax.psum_scatter(part, 'z', scatter_dimension=0, tiled=True)]
    all_to_all x0 -> x1, starting transfers between devices: none -> 3.31 us  [local(): lax.all_to_all(jnp.broadcast_to(y[None], (nx, rank, hidden)), 'x', 0, 0,...]
    pallas_call x1, Pallas kernels: 7.9 us -> 4.63 us  [gram_schmidt(): pl.pallas_call(gram_schmidt_kernel, out_shape=[jax.ShapeDtypeStruct((rank...]
    all_to_all x1, starting transfers between devices: 3.39 us -> 6.46 us  [local(): lax.all_to_all(jnp.broadcast_to(y[None], (ny, rank, hidden)), 'y', 0, 0,...]
    all_gather x1, waiting for transfers between devices: 49.4 us -> 46.5 us  [local(): rows = lax.all_gather(own, TENSOR, axis=0, tiled=True)]
  transfers between devices with their start and end apart: 3 -> 5, of which waited for: 3 -> 3; matrix products, arithmetic and copies ran while one was open for 3% -> 5% of each run, Pallas kernels for 7% -> 5%
where the time goes in v2:
time: 153 us; the launch traced here: 152 us
  waiting for transfers between devices  60.2 us (39%)
  blocking collectives  33.1 us (22%)
  Pallas kernels  21.2 us (14%)
  starting transfers between devices  14.9 us (10%)
  between operations  14.1 us (9%)
  local copies, waits for them, and re-layouts  7.05 us (5%)
  other arithmetic  1.53 us (1%)
    all_gather x1, waiting for transfers between devices, local(): rows = lax.all_gather(own, TENSOR, axis=0, tiled=True)  46.5 us
    all_to_all x1, blocking collectives, local(): p_parts = lax.all_to_all(p_local, DP, 0, 0, tiled=True)  18.4 us
    all_to_all x1, blocking collectives, local(): lax.all_to_all(jnp.broadcast_to(p_row[None], (replicas,) + p_row.shape),...  14.7 us
    pallas_call x1, Pallas kernels, backward(): pl.pallas_call(backward_kernel, in_specs=[pl.BlockSpec(memory_space=pltpu...  12.5 us
    reduce_scatter x1, waiting for transfers between devices, local(): dz_pair = lax.psum_scatter(part, 'z', scatter_dimension=0, tiled=True)  6.79 us
    all_to_all x1, starting transfers between devices, local(): lax.all_to_all(jnp.broadcast_to(y[None], (ny, rank, hidden)), 'y', 0, 0,...  6.46 us
    all_to_all x1, waiting for transfers between devices, local(): lax.all_to_all(jnp.broadcast_to(y[None], (ny, rank, hidden)), 'y', 0, 0,...  6.17 us
    ppermute x1, starting transfers between devices, local(): dz_peer = lax.ppermute(dz_pair, 'core', SWAP)  5.07 us
  transfers between devices with their start and end apart: 5, of which 3 were waited for; matrix products, arithmetic and copies ran while one was open for 5% of the time, Pallas kernels for 5%

profile of v2, /device:TPU:1, one launch (start us, length us, event | category | flops | bytes accessed | tf_op | source)
XLA Modules:
  0.0 152.0 jit_solution(13597816885243433042)
XLA Ops:
  7.2 0.0 copy-start.3
  7.2 0.0 all-gather.2.cloned.1.call-start
  7.2 0.7 all-gather.2.cloned.1.call-update
  7.9 0.0 reduce-scatter.2.cloned.1.call-start
  8.0 0.8 constant_dynamic-slice_fusion
  8.7 0.1 copy.20
  8.8 1.4 pad_maximum_fusion.film
  10.2 2.4 %copy.18 = bf16[1024,384]{0,1:T(8,128)(2,1)} copy(bf16[1024,384]{1,0:T(8,128)(2,1)} %param.9) | data formatting | bytes 1572864 | tf_op args[1]
  12.6 0.0 copy-done.3
  12.6 1.4 copy.17
  14.1 46.5 %all-gather.2.cloned.1.call-done.rows = bf16[1536,1024]{1,0:T(8,128)(2,1)} async-done(((bf16[96,1024]{1,0:T(8,128)(2,1)}), bf16[1536,1024]{1,0:T(8,128)(2,1)}) %all-gather.2.cloned.1.call-update) | async-done | bytes 3145744 | tf_op jit(solution)/shard_map/all_gather | solution.py:294
  60.6 12.5 %shard_map.127 = (bf16[1536,1024]{1,0:T(8,128)(2,1)}, f32[1536,384]{1,0:T(8,128)}, f32[32,1,1536]{2,1,0:T(1,128)}) custom-call(s32[4]{0:T(128)} %lengths.1, bf16[1536,1024]{1,0:T(8,128)(2,1)} %all-gather.2.cloned.1.call-done.rows, bf16[384,1536]{1,0:T(8,128)(2,1)} %bitcast.13, bf16[1536,384]{1,0:T(8,128)(2,1)} %weight.1, bf16[384,1024]{1,0:T(8,128)(2,1)} %bitcast.14, ...), custom_call_target="tpu_custom_call" | custom-call | flops 3623878656 | bytes 14680064 | tf_op jit(solution)/shard_map/pallas_call | solution.py:114
  73.1 0.0 copy-start.4
  73.1 0.0 reduce-scatter.2.cloned.1.call-update
  73.2 0.9 copy-done.4
  74.0 18.4 %all_to_all.20 = f32[32,1,1536]{2,1,0:T(1,128)S(1)} all-to-all(f32[32,1,1536]{2,1,0:T(1,128)S(1)} %copy-done.4), channel_id=1, replica_groups=mesh['x'=4,'y'=8,'z'=8,'core'=2] {'x','y'}, dimensions={0} | all-to-all | bytes 393216 | tf_op jit(solution)/shard_map/all_to_all | solution.py:311
  92.5 0.1 reduce_sum.21
  92.6 0.1 broadcast_in_dim.8
  92.7 14.7 %all_to_all.21.p_rows = f32[32,1,1536]{2,1,0:T(1,128)S(1)} all-to-all(f32[32,1,1536]{2,1,0:T(1,128)S(1)} %broadcast_in_dim.8), channel_id=1, replica_groups=mesh['x'=4,'y'=8,'z'=8,'core'=2] {'x','y'}, dimensions={0} | all-to-all | bytes 393216 | tf_op jit(solution)/shard_map/all_to_all | solution.py:313
  107.4 0.6 shard_map.130
  107.9 0.7 broadcast_in_dim.10
  108.6 3.3 %all-to-all-start.2 = ((bf16[4,32,384]{2,1,0:T(8,128)(2,1)}), bf16[4,32,384]{2,1,0:T(8,128)(2,1)S(1)}, u32[]{:S(2)}, u32[]{:S(2)}) async-start(bf16[4,32,384]{2,1,0:T(8,128)(2,1)} %broadcast_in_dim.10), calls=%async_computation.3 | async-start | bytes 196608 | tf_op jit(solution)/shard_map/all_to_all | solution.py:319
  111.9 6.8 %reduce-scatter.2.cloned.1.call-done = bf16[192,1024]{1,0:T(8,128)(2,1)} async-done(((bf16[1536,1024]{1,0:T(8,128)(2,1)}), bf16[192,1024]{1,0:T(8,128)(2,1)}) %reduce-scatter.2.cloned.1.call-update) | async-done | bytes 393232 | tf_op jit(solution)/shard_map/reduce_scatter | solution.py:304
  118.7 5.1 %collective-permute-start = (bf16[2,96,1024]{2,1,0:T(8,128)(2,1)}, bf16[2,96,1024]{2,1,0:T(8,128)(2,1)S(1)}, u32[]{:S(2)}, u32[]{:S(2)}) collective-permute-start(bf16[2,96,1024]{2,1,0:T(8,128)(2,1)} %bitcast.10), channel_id=1, source_target_pairs={{0,1},{1,0},{2,3},{3,2},{4,5},{5,4},{6,7},{7,6},{8,9},{9,8},{10,11... | collective-permute-start | bytes 1179656 | tf_op jit(solution)/shard_map/ppermute | solution.py:306
  123.8 0.0 all-to-all-done.2
  123.8 0.7 broadcast_in_dim.11
  124.5 6.5 %all-to-all-start.3 = ((bf16[8,32,384]{2,1,0:T(8,128)(2,1)}), bf16[8,32,384]{2,1,0:T(8,128)(2,1)S(1)}, u32[]{:S(2)}, u32[]{:S(2)}) async-start(bf16[8,32,384]{2,1,0:T(8,128)(2,1)} %broadcast_in_dim.11), calls=%async_computation.4 | async-start | bytes 393216 | tf_op jit(solution)/shard_map/all_to_all | solution.py:321
  131.0 4.6 %shard_map.129 = (f32[32,1536]{1,0:T(8,128)}, f32[32,128]{1,0:T(8,128)S(1)}, bf16[96,1536]{1,0:T(8,128)(2,1)S(1)}) custom-call(f32[32,1,1536]{2,1,0:T(1,128)S(1)} %all_to_all.21.p_rows), custom_call_target="tpu_custom_call" | custom-call | flops 6291456 | bytes 1048576 | tf_op jit(solution)/shard_map/pallas_call | solution.py:192
  135.6 6.2 %all-to-all-done.3.y_parts = bf16[8,32,384]{2,1,0:T(8,128)(2,1)S(1)} async-done(((bf16[8,32,384]{2,1,0:T(8,128)(2,1)}), bf16[8,32,384]{2,1,0:T(8,128)(2,1)S(1)}, u32[]{:S(2)}, u32[]{:S(2)}) %all-to-all-start.3) | async-done | bytes 196640 | tf_op jit(solution)/shard_map/all_to_all | solution.py:321
  141.8 2.5 %shard_map.131 = (f32[32,384]{1,0:T(8,128)}, bf16[1,1536,384]{2,1,0:T(8,128)(2,1)}) custom-call(bf16[8,32,384]{2,1,0:T(8,128)(2,1)S(1)} %all-to-all-done.3.y_parts, f32[32,128]{1,0:T(8,128)S(1)} %get-tuple-element.28.mix, bf16[96,1536]{1,0:T(8,128)(2,1)S(1)} %get-tuple-element.29.stack, f32[1536,384]{1,0:T(8,128)S(1)} %copy-done), custom_call_target="tpu_custom_call" | custom-call | flops 113246208 | bytes 4194304 | tf_op jit(solution)/shard_map/pallas_call | solution.py:230
  144.2 0.0 collective-permute-done.dz_peer
  144.2 1.0 shard_map.128
  (7 shorter events, 0.0 us)
Async XLA Ops:
  7.2 5.4 %copy-start.3 = (bf16[1536,384]{1,0:T(8,128)(2,1)S(1)}, bf16[1536,384]{1,0:T(8,128)(2,1)}, u32[]{:S(2)}) copy-start(bf16[1536,384]{1,0:T(8,128)(2,1)} %weight.1) | copy-start | bytes 3538948
  7.2 53.4 %all-gather.2.cloned.1.call-start = ((), (), s32[]{:S(2)}) async-start(), calls=%async_computation.5 | async-start | bytes 3342336 | tf_op jit(solution)/shard_map/all_gather | solution.py:294
  7.9 110.8 %reduce-scatter.2.cloned.1.call-start = ((), (), s32[]{:S(2)}) async-start(), calls=%async_computation.6 | async-start | bytes 3538944 | tf_op jit(solution)/shard_map/reduce_scatter | solution.py:304
  73.1 0.9 copy-start.4
  73.1 34.2 %copy-start = (f32[1536,384]{1,0:T(8,128)S(1)}, f32[1536,384]{1,0:T(8,128)}, u32[]{:S(2)}) copy-start(f32[1536,384]{1,0:T(8,128)} %get-tuple-element.27.moment) | copy-start | bytes 7077892
  108.6 15.2 %all-to-all-start.2 = ((bf16[4,32,384]{2,1,0:T(8,128)(2,1)}), bf16[4,32,384]{2,1,0:T(8,128)(2,1)S(1)}, u32[]{:S(2)}, u32[]{:S(2)}) async-start(bf16[4,32,384]{2,1,0:T(8,128)(2,1)} %broadcast_in_dim.10), calls=%async_computation.3 | async-start | bytes 196608 | tf_op jit(solution)/shard_map/all_to_all | solution.py:319
  118.7 25.5 %collective-permute-start = (bf16[2,96,1024]{2,1,0:T(8,128)(2,1)}, bf16[2,96,1024]{2,1,0:T(8,128)(2,1)S(1)}, u32[]{:S(2)}, u32[]{:S(2)}) collective-permute-start(bf16[2,96,1024]{2,1,0:T(8,128)(2,1)} %bitcast.10), channel_id=1, source_target_pairs={{0,1},{1,0},{2,3},{3,2},{4,5},{5,4},{6,7},{7,6},{8,9},{9,8},{10,11... | collective-permute-start | bytes 1179656 | tf_op jit(solution)/shard_map/ppermute | solution.py:306
  124.5 17.3 %all-to-all-start.3 = ((bf16[8,32,384]{2,1,0:T(8,128)(2,1)}), bf16[8,32,384]{2,1,0:T(8,128)(2,1)S(1)}, u32[]{:S(2)}, u32[]{:S(2)}) async-start(bf16[8,32,384]{2,1,0:T(8,128)(2,1)} %broadcast_in_dim.11), calls=%async_computation.4 | async-start | bytes 393216 | tf_op jit(solution)/shard_map/all_to_all | solution.py:321
  141.8 2.5 %copy-start.1 = (bf16[1024,96]{0,1:T(8,128)(2,1)S(1)}, bf16[1024,96]{0,1:T(8,128)(2,1)}, u32[]{:S(2)}) copy-start(bf16[1024,96]{0,1:T(8,128)(2,1)} %param.8) | copy-start | bytes 589828
  141.8 2.5 %copy-start.2 = (bf16[192,1024]{1,0:T(8,128)(2,1)S(1)}, bf16[192,1024]{1,0:T(8,128)(2,1)}, u32[]{:S(2)}) copy-start(bf16[192,1024]{1,0:T(8,128)(2,1)} %reduce-scatter.2.cloned.1.call-done) | copy-start | bytes 1179652
Sparse Core Ops, SparseCore 0:
  10.1 50.3 all-gather.1
  73.3 45.3 reduce-scatter.1

commit v3 on v2

--- a/solution.py
+++ b/solution.py
@@ -132,7 +132,7 @@
             pltpu.VMEM((width, hidden), F32),
             pltpu.SemaphoreType.DMA((3 * CHUNKS + 4,)),
         ],
-        compiler_params=pltpu.CompilerParams(vmem_limit_bytes=58 * MIB),
+        compiler_params=pltpu.CompilerParams(vmem_limit_bytes=50 * MIB),
         cost_estimate=pl.CostEstimate(
             flops=6 * tokens * width * hidden, bytes_accessed=14 * MIB, transcendentals=0
         ),
@@ -156,7 +156,7 @@
         out_shape=jax.ShapeDtypeStruct((rank, hidden), BF),
         compiler_params=pltpu.CompilerParams(vmem_limit_bytes=32 * MIB),
         cost_estimate=pl.CostEstimate(
-            flops=6 * rank * width * hidden, bytes_accessed=3 * MIB, transcendentals=0
+            flops=600_000_000, bytes_accessed=MIB, transcendentals=0
         ),
     )(p_rows, moment)
 
@@ -199,7 +199,7 @@
         scratch_shapes=[pltpu.VMEM((rank, width), F32), pltpu.VMEM((rank, width + 128), F32)],
         compiler_params=pltpu.CompilerParams(vmem_limit_bytes=16 * MIB),
         cost_estimate=pl.CostEstimate(
-            flops=4 * rank * rank * width, bytes_accessed=MIB, transcendentals=0
+            flops=5_300_000_000, bytes_accessed=MIB, transcendentals=0
         ),
     )(p_rows)
 
@@ -247,7 +247,7 @@
         scratch_shapes=[pltpu.VMEM((3 * rank, hidden), BF)],
         compiler_params=pltpu.CompilerParams(vmem_limit_bytes=16 * MIB),
         cost_estimate=pl.CostEstimate(
-            flops=6 * rank * width * hidden, bytes_accessed=4 * MIB, transcendentals=0
+            flops=2_900_000_000, bytes_accessed=4 * MIB, transcendentals=0
         ),
     )(y_parts, mix, stack, moment)
 
@@ -281,7 +281,7 @@
         ],
         compiler_params=pltpu.CompilerParams(vmem_limit_bytes=16 * MIB),
         cost_estimate=pl.CostEstimate(
-            flops=64 * tokens * width, bytes_accessed=MIB, transcendentals=0
+            flops=1_100_000_000, bytes_accessed=MIB, transcendentals=0
         ),
     )(core, dz_own, dz_peer, rows, scale_t)
 
@@ -303,21 +303,22 @@
 
     dz_pair = lax.psum_scatter(part, "z", scatter_dimension=0, tiled=True)
     dz_pair = dz_pair.reshape(2, col_width, -1)
-    dz_peer = lax.ppermute(dz_pair, "core", SWAP)
-    d_normed, d_scale, d_shift = film_gradients(
-        core.reshape(1), dz_pair, dz_peer, own, own_scale
-    )
-
     p_parts = lax.all_to_all(p_local, DP, 0, 0, tiled=True)
     p_row = jnp.sum(p_parts, axis=0)
     p_rows = lax.all_to_all(
         jnp.broadcast_to(p_row[None], (replicas,) + p_row.shape), DP, 0, 0, tiled=True
     )
     y = right_factor(p_rows, moment)
-    basis, mix, stack = gram_schmidt(p_rows)
     nx, ny = lax.axis_size("x"), lax.axis_size("y")
     y_x = lax.all_to_all(jnp.broadcast_to(y[None], (nx, rank, hidden)), "x", 0, 0, tiled=True)
     y = jnp.sum(y_x.astype(F32), axis=0).astype(BF)
+    p_late, _ = lax.optimization_barrier((p_rows, y))
+    basis, mix, stack = gram_schmidt(p_late)
+    dz_pair, _ = lax.optimization_barrier((dz_pair, mix))
+    dz_peer = lax.ppermute(dz_pair, "core", SWAP)
+    d_normed, d_scale, d_shift = film_gradients(
+        core.reshape(1), dz_pair, dz_peer, own, own_scale
+    )
     y_y = lax.all_to_all(jnp.broadcast_to(y[None], (ny, rank, hidden)), "y", 0, 0, tiled=True)
     q_new, new_error = finish(replicas, y_y, mix, stack, moment)
     return (d_normed.T, d_scale, d_shift, basis[None], q_new, new_error)

time: 153 us -> 141 us (0.922)
  waiting for transfers between devices: 60.2 us -> 49.5 us
  blocking collectives: 33.1 us -> 40.3 us
  starting transfers between devices: 14.9 us -> 9.69 us
  local copies, waits for them, and re-layouts: 7.05 us -> 5.43 us
    all_to_all x0 -> x1, blocking collectives: none -> 7.03 us  [local(): lax.all_to_all(jnp.broadcast_to(y[None], (nx, rank, hidden)), 'x', 0, 0,...]
    reduce_scatter x1, waiting for transfers between devices: 6.79 us -> 0.01 us  [local(): dz_pair = lax.psum_scatter(part, 'z', scatter_dimension=0, tiled=True)]
    all_to_all x1, waiting for transfers between devices: 6.17 us -> 0.01 us  [local(): lax.all_to_all(jnp.broadcast_to(y[None], (ny, rank, hidden)), 'y', 0, 0,...]
    all_to_all x1 -> x0, starting transfers between devices: 3.31 us -> none  [local(): lax.all_to_all(jnp.broadcast_to(y[None], (nx, rank, hidden)), 'x', 0, 0,...]
    all_to_all x1, starting transfers between devices: 6.46 us -> 3.39 us  [local(): lax.all_to_all(jnp.broadcast_to(y[None], (ny, rank, hidden)), 'y', 0, 0,...]
    all_gather x1, waiting for transfers between devices: 46.5 us -> 48.8 us  [local(): rows = lax.all_gather(own, TENSOR, axis=0, tiled=True)]
    unnamed x13 -> x19, local copies, waits for them, and re-layouts: 4.84 us -> 3.86 us
  transfers between devices with their start and end apart: 5 -> 4, of which waited for: 3 -> 1; matrix products, arithmetic and copies ran while one was open for 5% -> 3% of each run, Pallas kernels for 5% -> 5%
where the time goes in v3:
time: 141 us; the launch traced here: 140 us
  waiting for transfers between devices  49.5 us (35%)
  blocking collectives  40.3 us (29%)
  Pallas kernels  20.2 us (14%)
  between operations  14.2 us (10%)
  starting transfers between devices  9.69 us (7%)
  local copies, waits for them, and re-layouts  5.43 us (4%)
    all_gather x1, waiting for transfers between devices, local(): rows = lax.all_gather(own, TENSOR, axis=0, tiled=True)  48.8 us
    all_to_all x1, blocking collectives, local(): p_parts = lax.all_to_all(p_local, DP, 0, 0, tiled=True)  18.6 us
    all_to_all x1, blocking collectives, local(): lax.all_to_all(jnp.broadcast_to(p_row[None], (replicas,) + p_row.shape),...  14.7 us
    pallas_call x1, Pallas kernels, backward(): pl.pallas_call(backward_kernel, in_specs=[pl.BlockSpec(memory_space=pltpu...  11.5 us
    all_to_all x1, blocking collectives, local(): lax.all_to_all(jnp.broadcast_to(y[None], (nx, rank, hidden)), 'x', 0, 0,...  7.03 us
    ppermute x1, starting transfers between devices, local(): dz_peer = lax.ppermute(dz_pair, 'core', SWAP)  6.22 us
    pallas_call x1, Pallas kernels, gram_schmidt(): pl.pallas_call(gram_schmidt_kernel, out_shape=[jax.ShapeDtypeStruct((rank...  4.64 us
    unnamed x19, local copies, waits for them, and re-layouts  3.86 us
  transfers between devices with their start and end apart: 4, of which 1 were waited for; matrix products, arithmetic and copies ran while one was open for 3% of the time, Pallas kernels for 5%

profile of v3, /device:TPU:1, one launch (start us, length us, event | category | flops | bytes accessed | tf_op | source)
XLA Modules:
  0.0 140.2 jit_solution(15030487014354039245)
XLA Ops:
  7.2 0.0 copy-start.1
  7.2 0.0 all-gather.2.cloned.1.call-start
  7.2 0.7 all-gather.2.cloned.1.call-update
  7.9 0.0 reduce-scatter.2.cloned.1.call-start
  8.0 0.8 constant_dynamic-slice_fusion
  8.7 0.1 copy.20
  8.8 0.8 pad_maximum_fusion.film
  9.6 1.4 %copy.18 = bf16[1024,384]{0,1:T(8,128)(2,1)S(1)} copy(bf16[1024,384]{1,0:T(8,128)(2,1)} %param.9) | data formatting | bytes 1572864 | tf_op args[1]
  11.0 0.0 copy-done.1
  11.0 0.0 copy-start.4
  11.0 0.0 copy-start.5
  11.1 0.6 copy.17
  11.7 48.8 %all-gather.2.cloned.1.call-done.rows = bf16[1536,1024]{1,0:T(8,128)(2,1)} async-done(((bf16[96,1024]{1,0:T(8,128)(2,1)}), bf16[1536,1024]{1,0:T(8,128)(2,1)}) %all-gather.2.cloned.1.call-update) | async-done | bytes 3145744 | tf_op jit(solution)/shard_map/all_gather | solution.py:294
  60.6 11.5 %shard_map.127 = (bf16[1536,1024]{1,0:T(8,128)(2,1)}, f32[1536,384]{1,0:T(8,128)}, f32[32,1,1536]{2,1,0:T(1,128)S(1)}) custom-call(s32[4]{0:T(128)S(1)} %copy-done.5, bf16[1536,1024]{1,0:T(8,128)(2,1)} %all-gather.2.cloned.1.call-done.rows, bf16[384,1536]{1,0:T(8,128)(2,1)S(1)} %bitcast.8, bf16[1536,384]{1,0:T(8,128)(2,1)S(1)} %copy-done.1, ...), custom_call_target="tpu_custom_call" | custom-call | flops 3623878656 | bytes 14680064 | tf_op jit(solution)/shard_map/pallas_call | solution.py:114
  72.1 0.0 reduce-scatter.2.cloned.1.call-update
  72.1 18.6 %all_to_all.20 = f32[32,1,1536]{2,1,0:T(1,128)S(1)} all-to-all(f32[32,1,1536]{2,1,0:T(1,128)S(1)} %get-tuple-element.23), channel_id=1, replica_groups=mesh['x'=4,'y'=8,'z'=8,'core'=2] {'x','y'}, dimensions={0} | all-to-all | bytes 393216 | tf_op jit(solution)/shard_map/all_to_all | solution.py:306
  90.7 0.1 reduce_sum.21
  90.9 0.1 broadcast_in_dim.8
  91.0 14.7 %all_to_all.21.p_rows = f32[32,1,1536]{2,1,0:T(1,128)S(1)} all-to-all(f32[32,1,1536]{2,1,0:T(1,128)S(1)} %broadcast_in_dim.8), channel_id=1, replica_groups=mesh['x'=4,'y'=8,'z'=8,'core'=2] {'x','y'}, dimensions={0} | all-to-all | bytes 393216 | tf_op jit(solution)/shard_map/all_to_all | solution.py:308
  105.6 0.6 shard_map.128
  106.2 7.0 %all_to_all.22 = bf16[4,32,384]{2,1,0:T(8,128)(2,1)S(1)} all-to-all(bf16[4,32,384]{2,1,0:T(8,128)(2,1)S(1)} %broadcast_in_dim.9), channel_id=1, replica_groups=mesh['x'=4,'y'=8,'z'=8,'core'=2] {'x'}, dimensions={0} | all-to-all | bytes 196608 | tf_op jit(solution)/shard_map/all_to_all | solution.py:313
  113.3 0.7 broadcast_in_dim.11
  114.0 3.4 %all-to-all-start.3 = ((bf16[8,32,384]{2,1,0:T(8,128)(2,1)}), bf16[8,32,384]{2,1,0:T(8,128)(2,1)S(1)}, u32[]{:S(2)}, u32[]{:S(2)}) async-start(bf16[8,32,384]{2,1,0:T(8,128)(2,1)} %broadcast_in_dim.11), calls=%async_computation.4 | async-start | bytes 393216 | tf_op jit(solution)/shard_map/all_to_all | solution.py:322
  117.4 4.6 %shard_map.129 = (f32[32,1536]{1,0:T(8,128)}, f32[32,128]{1,0:T(8,128)S(1)}, bf16[96,1536]{1,0:T(8,128)(2,1)S(1)}) custom-call(f32[32,1,1536]{2,1,0:T(1,128)S(1)} %all_to_all.21.p_rows), custom_call_target="tpu_custom_call" | custom-call | flops 5299999744 | bytes 1048576 | tf_op jit(solution)/shard_map/pallas_call | solution.py:192
  122.0 0.7 copy-done.6
  122.7 6.2 %collective-permute-start = (bf16[2,96,1024]{2,1,0:T(8,128)(2,1)}, bf16[2,96,1024]{2,1,0:T(8,128)(2,1)S(1)}, u32[]{:S(2)}, u32[]{:S(2)}) collective-permute-start(bf16[2,96,1024]{2,1,0:T(8,128)(2,1)} %bitcast.13), channel_id=1, source_target_pairs={{0,1},{1,0},{2,3},{3,2},{4,5},{5,4},{6,7},{7,6},{8,9},{9,8},{10,11... | collective-permute-start | bytes 1179656 | tf_op jit(solution)/shard_map/ppermute | solution.py:318
  128.9 0.0 all-to-all-done.3.y_parts
  129.0 0.0 copy-start.7
  129.0 1.0 copy-done.7
  129.9 2.5 %shard_map.131 = (f32[32,384]{1,0:T(8,128)}, bf16[1,1536,384]{2,1,0:T(8,128)(2,1)}) custom-call(bf16[8,32,384]{2,1,0:T(8,128)(2,1)S(1)} %all-to-all-done.3.y_parts, f32[32,128]{1,0:T(8,128)S(1)} %get-tuple-element.26.mix, bf16[96,1536]{1,0:T(8,128)(2,1)S(1)} %copy-done.7, f32[1536,384]{1,0:T(8,128)S(1)} %copy-done), custom_call_target="tpu_custom_call" | custom-call | flops 2900000000 | bytes 4194304 | tf_op jit(solution)/shard_map/pallas_call | solution.py:230
  132.4 0.0 collective-permute-done.dz_peer
  132.4 1.0 shard_map.130
  (12 shorter events, 0.0 us)
Async XLA Ops:
  7.2 3.9 %copy-start.1 = (bf16[1536,384]{1,0:T(8,128)(2,1)S(1)}, bf16[1536,384]{1,0:T(8,128)(2,1)}, u32[]{:S(2)}) copy-start(bf16[1536,384]{1,0:T(8,128)(2,1)} %weight.1) | copy-start | bytes 3538948
  7.2 53.4 %all-gather.2.cloned.1.call-start = ((), (), s32[]{:S(2)}) async-start(), calls=%async_computation.5 | async-start | bytes 3342336 | tf_op jit(solution)/shard_map/all_gather | solution.py:294
  7.9 114.8 %reduce-scatter.2.cloned.1.call-start = ((), (), s32[]{:S(2)}) async-start(), calls=%async_computation.6 | async-start | bytes 3538944 | tf_op jit(solution)/shard_map/reduce_scatter | solution.py:304
  11.0 49.5 %copy-start.4 = (f32[32,384]{1,0:T(8,128)S(1)}, f32[32,384]{1,0:T(8,128)}, u32[]{:S(2)}) copy-start(f32[32,384]{1,0:T(8,128)} %q_init.1) | copy-start | bytes 147460
  11.0 49.5 %copy-start.5 = (s32[4]{0:T(128)S(1)}, s32[4]{0:T(128)}, u32[]{:S(2)}) copy-start(s32[4]{0:T(128)} %lengths.1) | copy-start | bytes 52
  72.1 33.5 %copy-start = (f32[1536,384]{1,0:T(8,128)S(1)}, f32[1536,384]{1,0:T(8,128)}, u32[]{:S(2)}) copy-start(f32[1536,384]{1,0:T(8,128)} %get-tuple-element.24.moment) | copy-start | bytes 7077892
  114.0 15.0 %all-to-all-start.3 = ((bf16[8,32,384]{2,1,0:T(8,128)(2,1)}), bf16[8,32,384]{2,1,0:T(8,128)(2,1)S(1)}, u32[]{:S(2)}, u32[]{:S(2)}) async-start(bf16[8,32,384]{2,1,0:T(8,128)(2,1)} %broadcast_in_dim.11), calls=%async_computation.4 | async-start | bytes 393216 | tf_op jit(solution)/shard_map/all_to_all | solution.py:322
  122.0 0.7 copy-start.6
  122.7 9.7 %collective-permute-start = (bf16[2,96,1024]{2,1,0:T(8,128)(2,1)}, bf16[2,96,1024]{2,1,0:T(8,128)(2,1)S(1)}, u32[]{:S(2)}, u32[]{:S(2)}) collective-permute-start(bf16[2,96,1024]{2,1,0:T(8,128)(2,1)} %bitcast.13), channel_id=1, source_target_pairs={{0,1},{1,0},{2,3},{3,2},{4,5},{5,4},{6,7},{7,6},{8,9},{9,8},{10,11... | collective-permute-start | bytes 1179656 | tf_op jit(solution)/shard_map/ppermute | solution.py:318
  129.0 1.0 copy-start.7
  129.9 2.5 %copy-start.2 = (bf16[1024,96]{0,1:T(8,128)(2,1)S(1)}, bf16[1024,96]{0,1:T(8,128)(2,1)}, u32[]{:S(2)}) copy-start(bf16[1024,96]{0,1:T(8,128)(2,1)} %param.8) | copy-start | bytes 589828
  129.9 2.5 %copy-start.3 = (bf16[192,1024]{1,0:T(8,128)(2,1)S(1)}, bf16[192,1024]{1,0:T(8,128)(2,1)}, u32[]{:S(2)}) copy-start(bf16[192,1024]{1,0:T(8,128)(2,1)} %reduce-scatter.2.cloned.1.call-done) | copy-start | bytes 1179652
Sparse Core Ops, SparseCore 0:
  10.1 50.3 all-gather.1
  72.3 45.2 reduce-scatter.1

commit v4 on v3

--- a/solution.py
+++ b/solution.py
@@ -18,6 +18,7 @@
 TN = (((0,), (0,)), ((), ()))
 MIB = 1024 * 1024
 CHUNKS = 3
+HALVES = 2
 IN_VMEM = pl.BlockSpec(memory_space=pltpu.VMEM)
 IN_HBM = pl.BlockSpec(memory_space=pltpu.HBM)
 
@@ -60,31 +61,27 @@
     get_error = fetch(error.at[0], err_buf)
 
     film_t = film[...].T
-    u = None
     for c in range(CHUNKS):
         cut = slice(c * step, (c + 1) * step)
         get_rows[c].wait()
-        z = jnp.concatenate(
-            [
-                (
-                    row_buf[cut, k * SEQ:(k + 1) * SEQ].astype(F32) * film_t[cut, k:k + 1]
-                    + film_t[cut, samples + k:samples + k + 1]
-                ).astype(BF)
-                for k in range(samples)
-            ],
-            axis=1,
+        for k in range(samples):
+            z_buf[cut, k * SEQ:(k + 1) * SEQ] = (
+                row_buf[cut, k * SEQ:(k + 1) * SEQ].astype(F32) * film_t[cut, k:k + 1]
+                + film_t[cut, samples + k:samples + k + 1]
+            ).astype(BF)
+    get_wt.wait()
+    get_cot.wait()
+    position = lax.broadcasted_iota(jnp.int32, (1, SEQ), 1)
+    halves = []
+    for h in range(HALVES):
+        span = samples // HALVES
+        cols = slice(h * span * SEQ, (h + 1) * span * SEQ)
+        u = mm(wt_buf[...], z_buf[:, cols], NN)
+        valid = jnp.concatenate(
+            [(position < lengths[k]).astype(F32) for k in range(h * span, (h + 1) * span)], axis=1
         )
-        z_buf[cut, :] = z
-        if c == 0:
-            get_wt.wait()
-        term = mm(wt_buf[:, cut], z, NN)
-        u = term if u is None else u + term
-    position = lax.broadcasted_iota(jnp.int32, (1, SEQ), 1)
-    valid = jnp.concatenate(
-        [(position < lengths[k]).astype(F32) for k in range(samples)], axis=1
-    )
-    get_cot.wait()
-    d_pre = (cot_buf[...].astype(F32) * gelu_slope(u) * valid).astype(BF)
+        halves.append((cot_buf[:, cols].astype(F32) * gelu_slope(u) * valid).astype(BF))
+    d_pre = jnp.concatenate(halves, axis=1)
     get_w.wait()
     puts = []
     for c in range(CHUNKS):
@@ -94,6 +91,7 @@
     get_error.wait()
     q_hi, q_lo = split(q_init[...])
     q_both = jnp.concatenate([q_hi, q_lo], axis=0)
+    p_parts = []
     for c in range(CHUNKS):
         cut = slice(c * step, (c + 1) * step)
         total = mm(z_buf[cut, :], d_pre, NT) + err_buf[cut, :].astype(F32)
@@ -102,8 +100,11 @@
         m_hi, m_lo = split(total)
         first = mm(q_both, m_hi, NT)
         p = first[:rank] + first[rank:] + mm(q_hi, m_lo, NT)
-        for k in range(rank):
-            p_out[k, :, cut] = p[k:k + 1]
+        p_parts.append(p)
+    p = jnp.concatenate(p_parts, axis=1)
+    half = width // 2
+    for k in range(rank):
+        p_out[k] = jnp.concatenate([p[k:k + 1, :half], p[k:k + 1, half:]], axis=0).astype(BF)
     for put in puts:
         put.wait()
 
@@ -119,7 +120,7 @@
         out_shape=[
             jax.ShapeDtypeStruct((width, tokens), BF),
             jax.ShapeDtypeStruct((width, hidden), F32),
-            jax.ShapeDtypeStruct((rank, 1, width), F32),
+            jax.ShapeDtypeStruct((rank, 2, width // 2), BF),
         ],
         scratch_shapes=[
             pltpu.VMEM((width, tokens), BF),
@@ -141,11 +142,12 @@
 
 def right_kernel(p_rows, moment, y_out):
     rank = p_rows.shape[0]
-    p = jnp.concatenate([p_rows[k] for k in range(rank)], axis=0)
-    p_hi, p_lo = split(p)
+    rows = [p_rows[k].astype(F32) for k in range(rank)]
+    p = jnp.concatenate(
+        [jnp.concatenate([row[h:h + 1] for row in rows], axis=0) for h in range(2)], axis=1
+    ).astype(BF)
     m_hi, m_lo = split(moment[...])
-    first = mm(jnp.concatenate([p_hi, p_lo], axis=0), m_hi, NN)
-    y_out[...] = (first[:rank] + first[rank:] + mm(p_hi, m_lo, NN)).astype(BF)
+    y_out[...] = (mm(p, m_hi, NN) + mm(p, m_lo, NN)).astype(BF)
 
 
 def right_factor(p_rows, moment):
@@ -162,10 +164,13 @@
 
 
 def gram_schmidt_kernel(p_rows, basis_out, mix_out, stack_out, p, work):
-    rank, _, width = p_rows.shape
+    rank, _, half = p_rows.shape
+    width = 2 * half
     for k in range(rank):
-        p[k:k + 1, :] = p_rows[k]
-        work[k:k + 1, :width] = p_rows[k]
+        row = p_rows[k].astype(F32)
+        row = jnp.concatenate([row[:1], row[1:]], axis=1)
+        p[k:k + 1, :] = row
+        work[k:k + 1, :width] = row
     eye_row = lax.broadcasted_iota(jnp.int32, (rank, 128), 0)
     eye_col = lax.broadcasted_iota(jnp.int32, (rank, 128), 1)
     work[:, width:] = (eye_row == eye_col).astype(F32)
@@ -188,7 +193,8 @@
 
 
 def gram_schmidt(p_rows):
-    rank, _, width = p_rows.shape
+    rank, _, half = p_rows.shape
+    width = 2 * half
     return pl.pallas_call(
         gram_schmidt_kernel,
         out_shape=[
@@ -204,50 +210,49 @@
     )(p_rows)
 
 
-def finish_kernel(replicas, y_parts, mix, stack, moment, q_out, error_out, q_buf):
+def finish_kernel(replicas, y_parts, mix, stack, moment, q_out, error_out, buf, sems):
     rank = q_out.shape[0]
-
-    @pl.when(pl.program_id(0) == 0)
-    def _():
-        y = y_parts[0].astype(F32)
-        for k in range(1, y_parts.shape[0]):
-            y = y + y_parts[k].astype(F32)
-        y_hi, y_lo = split(y * (1.0 / replicas))
-        a_hi, a_lo = split(mix[:, :rank])
-        q_new = mm(a_hi, y_hi, NN) + mm(a_lo, y_hi, NN) + mm(a_hi, y_lo, NN)
-        q_out[...] = q_new
-        q_hi, q_lo = split(q_new)
-        q_buf[...] = jnp.concatenate([q_hi, q_hi, q_lo], axis=0)
-
-    averaged = mm(stack[...], q_buf[...], TN)
-    error_out[0] = (moment[...] - averaged).astype(BF)
+    y = y_parts[0].astype(F32)
+    for k in range(1, y_parts.shape[0]):
+        y = y + y_parts[k].astype(F32)
+    y_hi, y_lo = split(y * (1.0 / replicas))
+    a_hi, a_lo = split(mix[:, :rank])
+    q_new = mm(a_hi, y_hi, NN) + mm(a_lo, y_hi, NN) + mm(a_hi, y_lo, NN)
+    q_out[...] = q_new
+    q_hi, q_lo = split(q_new)
+    q_stack = jnp.concatenate([q_hi, q_hi, q_lo], axis=0)
+    step = moment.shape[0] // CHUNKS
+    puts = []
+    for c in range(CHUNKS):
+        cut = slice(c * step, (c + 1) * step)
+        averaged = mm(stack[:, cut], q_stack, TN)
+        buf[cut, :] = (moment[cut, :] - averaged).astype(BF)
+        put = pltpu.make_async_copy(
+            buf.at[pl.ds(c * step, step)], error_out.at[0, pl.ds(c * step, step)], sems.at[c]
+        )
+        put.start()
+        puts.append(put)
+    for put in puts:
+        put.wait()
 
 
 def finish(replicas, y_parts, mix, stack, moment):
     width, hidden = moment.shape
     rank = mix.shape[0]
-    block = width // 4
     return pl.pallas_call(
         functools.partial(finish_kernel, replicas),
-        grid=(4,),
-        in_specs=[
-            pl.BlockSpec(y_parts.shape, lambda i: (0, 0, 0)),
-            pl.BlockSpec(mix.shape, lambda i: (0, 0)),
-            pl.BlockSpec((3 * rank, block), lambda i: (0, i)),
-            pl.BlockSpec((block, hidden), lambda i: (i, 0)),
-        ],
-        out_specs=[
-            pl.BlockSpec((rank, hidden), lambda i: (0, 0)),
-            pl.BlockSpec((1, block, hidden), lambda i: (0, i, 0)),
-        ],
+        out_specs=[IN_VMEM, IN_HBM],
         out_shape=[
             jax.ShapeDtypeStruct((rank, hidden), F32),
             jax.ShapeDtypeStruct((1, width, hidden), BF),
         ],
-        scratch_shapes=[pltpu.VMEM((3 * rank, hidden), BF)],
+        scratch_shapes=[
+            pltpu.VMEM((width, hidden), BF),
+            pltpu.SemaphoreType.DMA((CHUNKS,)),
+        ],
         compiler_params=pltpu.CompilerParams(vmem_limit_bytes=16 * MIB),
         cost_estimate=pl.CostEstimate(
-            flops=2_900_000_000, bytes_accessed=4 * MIB, transcendentals=0
+            flops=2_500_000_000, bytes_accessed=4 * MIB, transcendentals=0
         ),
     )(y_parts, mix, stack, moment)
 
@@ -304,7 +309,7 @@
     dz_pair = lax.psum_scatter(part, "z", scatter_dimension=0, tiled=True)
     dz_pair = dz_pair.reshape(2, col_width, -1)
     p_parts = lax.all_to_all(p_local, DP, 0, 0, tiled=True)
-    p_row = jnp.sum(p_parts, axis=0)
+    p_row = jnp.sum(p_parts.astype(F32), axis=0).astype(BF)
     p_rows = lax.all_to_all(
         jnp.broadcast_to(p_row[None], (replicas,) + p_row.shape), DP, 0, 0, tiled=True
     )

time: 141 us -> 137 us (0.972)
  blocking collectives: 40.3 us -> 37.8 us
    all_to_all x1, blocking collectives: 14.7 us -> 12.6 us  [local(): lax.all_to_all(jnp.broadcast_to(p_row[None], (replicas,) + p_row.shape),...]
where the time goes in v4:
time: 137 us; the launch traced here: 136 us
  waiting for transfers between devices  49.5 us (36%)
  blocking collectives  37.8 us (28%)
  Pallas kernels  19.1 us (14%)
  between operations  14.2 us (10%)
  starting transfers between devices  9.31 us (7%)
  local copies, waits for them, and re-layouts  5.38 us (4%)
    all_gather x1, waiting for transfers between devices, local(): rows = lax.all_gather(own, TENSOR, axis=0, tiled=True)  48.8 us
    all_to_all x1, blocking collectives, local(): p_parts = lax.all_to_all(p_local, DP, 0, 0, tiled=True)  18.2 us
    all_to_all x1, blocking collectives, local(): lax.all_to_all(jnp.broadcast_to(p_row[None], (replicas,) + p_row.shape),...  12.6 us
    pallas_call x1, Pallas kernels, backward(): pl.pallas_call(backward_kernel, in_specs=[pl.BlockSpec(memory_space=pltpu...  10.8 us
    all_to_all x1, blocking collectives, local(): lax.all_to_all(jnp.broadcast_to(y[None], (nx, rank, hidden)), 'x', 0, 0,...  7.03 us
    ppermute x1, starting transfers between devices, local(): dz_peer = lax.ppermute(dz_pair, 'core', SWAP)  5.84 us
    pallas_call x1, Pallas kernels, gram_schmidt(): pl.pallas_call(gram_schmidt_kernel, out_shape=[jax.ShapeDtypeStruct((rank...  4.66 us
    unnamed x19, local copies, waits for them, and re-layouts  3.86 us
  transfers between devices with their start and end apart: 4, of which 1 were waited for; matrix products, arithmetic and copies ran while one was open for 3% of the time, Pallas kernels for 5%

profile of v4, /device:TPU:1, one launch (start us, length us, event | category | flops | bytes accessed | tf_op | source)
XLA Modules:
  0.0 136.3 jit_solution(4035011430072368168)
XLA Ops:
  7.2 0.0 copy-start.1
  7.2 0.0 all-gather.2.cloned.1.call-start
  7.2 0.7 all-gather.2.cloned.1.call-update
  7.9 0.0 reduce-scatter.2.cloned.1.call-start
  8.0 0.8 constant_dynamic-slice_fusion
  8.7 0.1 copy.20
  8.8 0.8 pad_maximum_fusion.film
  9.6 1.4 %copy.18 = bf16[1024,384]{0,1:T(8,128)(2,1)S(1)} copy(bf16[1024,384]{1,0:T(8,128)(2,1)} %param.9) | data formatting | bytes 1572864 | tf_op args[1]
  11.0 0.0 copy-done.1
  11.0 0.0 copy-start.4
  11.0 0.0 copy-start.5
  11.1 0.6 copy.17
  11.7 48.8 %all-gather.2.cloned.1.call-done.rows = bf16[1536,1024]{1,0:T(8,128)(2,1)} async-done(((bf16[96,1024]{1,0:T(8,128)(2,1)}), bf16[1536,1024]{1,0:T(8,128)(2,1)}) %all-gather.2.cloned.1.call-update) | async-done | bytes 3145744 | tf_op jit(solution)/shard_map/all_gather | solution.py:299
  60.6 10.8 %shard_map.127 = (bf16[1536,1024]{1,0:T(8,128)(2,1)}, f32[1536,384]{1,0:T(8,128)}, bf16[32,2,768]{2,1,0:T(2,128)(2,1)S(1)}) custom-call(s32[4]{0:T(128)S(1)} %copy-done.5, bf16[1536,1024]{1,0:T(8,128)(2,1)} %all-gather.2.cloned.1.call-done.rows, bf16[384,1536]{1,0:T(8,128)(2,1)S(1)} %bitcast.8, bf16[1536,384]{1,0:T(8,128)(2,1)S(1)} %copy-done.1, ...), custom_call_target="tpu_custom_call" | custom-call | flops 3623878656 | bytes 14680064 | tf_op jit(solution)/shard_map/pallas_call | solution.py:115
  71.4 0.0 reduce-scatter.2.cloned.1.call-update
  71.4 18.2 %all_to_all.20 = bf16[32,2,768]{2,1,0:T(2,128)(2,1)S(1)} all-to-all(bf16[32,2,768]{2,1,0:T(2,128)(2,1)S(1)} %get-tuple-element.23), channel_id=1, replica_groups=mesh['x'=4,'y'=8,'z'=8,'core'=2] {'x','y'}, dimensions={0} | all-to-all | bytes 196608 | tf_op jit(solution)/shard_map/all_to_all | solution.py:311
  89.7 0.1 reduce_sum.24
  89.8 0.1 broadcast_in_dim.8
  89.8 12.6 %all_to_all.21.p_rows = bf16[32,2,768]{2,1,0:T(2,128)(2,1)S(1)} all-to-all(bf16[32,2,768]{2,1,0:T(2,128)(2,1)S(1)} %broadcast_in_dim.8), channel_id=1, replica_groups=mesh['x'=4,'y'=8,'z'=8,'core'=2] {'x','y'}, dimensions={0} | all-to-all | bytes 196608 | tf_op jit(solution)/shard_map/all_to_all | solution.py:313
  102.4 0.6 shard_map.128
  103.0 7.0 %all_to_all.22 = bf16[4,32,384]{2,1,0:T(8,128)(2,1)S(1)} all-to-all(bf16[4,32,384]{2,1,0:T(8,128)(2,1)S(1)} %broadcast_in_dim.9), channel_id=1, replica_groups=mesh['x'=4,'y'=8,'z'=8,'core'=2] {'x'}, dimensions={0} | all-to-all | bytes 196608 | tf_op jit(solution)/shard_map/all_to_all | solution.py:318
  110.0 0.7 broadcast_in_dim.11
  110.7 3.4 %all-to-all-start.3 = ((bf16[8,32,384]{2,1,0:T(8,128)(2,1)}), bf16[8,32,384]{2,1,0:T(8,128)(2,1)S(1)}, u32[]{:S(2)}, u32[]{:S(2)}) async-start(bf16[8,32,384]{2,1,0:T(8,128)(2,1)} %broadcast_in_dim.11), calls=%async_computation.4 | async-start | bytes 393216 | tf_op jit(solution)/shard_map/all_to_all | solution.py:327
  114.1 4.7 %shard_map.129 = (f32[32,1536]{1,0:T(8,128)}, f32[32,128]{1,0:T(8,128)S(1)}, bf16[96,1536]{1,0:T(8,128)(2,1)S(1)}) custom-call(bf16[32,2,768]{2,1,0:T(2,128)(2,1)S(1)} %all_to_all.21.p_rows), custom_call_target="tpu_custom_call" | custom-call | flops 5299999744 | bytes 1048576 | tf_op jit(solution)/shard_map/pallas_call | solution.py:198
  118.8 0.7 copy-done.6
  119.5 5.8 %collective-permute-start = (bf16[2,96,1024]{2,1,0:T(8,128)(2,1)}, bf16[2,96,1024]{2,1,0:T(8,128)(2,1)S(1)}, u32[]{:S(2)}, u32[]{:S(2)}) collective-permute-start(bf16[2,96,1024]{2,1,0:T(8,128)(2,1)} %bitcast.13), channel_id=1, source_target_pairs={{0,1},{1,0},{2,3},{3,2},{4,5},{5,4},{6,7},{7,6},{8,9},{9,8},{10,11... | collective-permute-start | bytes 1179656 | tf_op jit(solution)/shard_map/ppermute | solution.py:323
  125.3 0.0 all-to-all-done.3.y_parts
  125.4 0.0 copy-start.7
  125.4 1.0 copy-done.7
  126.3 2.1 %shard_map.131 = (f32[32,384]{1,0:T(8,128)}, bf16[1,1536,384]{2,1,0:T(8,128)(2,1)}) custom-call(bf16[8,32,384]{2,1,0:T(8,128)(2,1)S(1)} %all-to-all-done.3.y_parts, f32[32,128]{1,0:T(8,128)S(1)} %get-tuple-element.26.mix, bf16[96,1536]{1,0:T(8,128)(2,1)S(1)} %copy-done.7, f32[1536,384]{1,0:T(8,128)S(1)} %copy-done), custom_call_target="tpu_custom_call" | custom-call | flops 2500000000 | bytes 4194304 | tf_op jit(solution)/shard_map/pallas_call | solution.py:242
  128.4 0.0 collective-permute-done.dz_peer
  128.5 1.0 shard_map.130
  (12 shorter events, 0.0 us)
Async XLA Ops:
  7.2 3.9 %copy-start.1 = (bf16[1536,384]{1,0:T(8,128)(2,1)S(1)}, bf16[1536,384]{1,0:T(8,128)(2,1)}, u32[]{:S(2)}) copy-start(bf16[1536,384]{1,0:T(8,128)(2,1)} %weight.1) | copy-start | bytes 3538948
  7.2 53.4 %all-gather.2.cloned.1.call-start = ((), (), s32[]{:S(2)}) async-start(), calls=%async_computation.5 | async-start | bytes 3342336 | tf_op jit(solution)/shard_map/all_gather | solution.py:299
  7.9 111.6 %reduce-scatter.2.cloned.1.call-start = ((), (), s32[]{:S(2)}) async-start(), calls=%async_computation.6 | async-start | bytes 3538944 | tf_op jit(solution)/shard_map/reduce_scatter | solution.py:309
  11.0 49.5 %copy-start.4 = (f32[32,384]{1,0:T(8,128)S(1)}, f32[32,384]{1,0:T(8,128)}, u32[]{:S(2)}) copy-start(f32[32,384]{1,0:T(8,128)} %q_init.1) | copy-start | bytes 147460
  11.0 49.5 %copy-start.5 = (s32[4]{0:T(128)S(1)}, s32[4]{0:T(128)}, u32[]{:S(2)}) copy-start(s32[4]{0:T(128)} %lengths.1) | copy-start | bytes 52
  71.4 31.0 %copy-start = (f32[1536,384]{1,0:T(8,128)S(1)}, f32[1536,384]{1,0:T(8,128)}, u32[]{:S(2)}) copy-start(f32[1536,384]{1,0:T(8,128)} %get-tuple-element.24.moment) | copy-start | bytes 7077892
  110.7 14.6 %all-to-all-start.3 = ((bf16[8,32,384]{2,1,0:T(8,128)(2,1)}), bf16[8,32,384]{2,1,0:T(8,128)(2,1)S(1)}, u32[]{:S(2)}, u32[]{:S(2)}) async-start(bf16[8,32,384]{2,1,0:T(8,128)(2,1)} %broadcast_in_dim.11), calls=%async_computation.4 | async-start | bytes 393216 | tf_op jit(solution)/shard_map/all_to_all | solution.py:327
  118.8 0.7 copy-start.6
  119.5 8.9 %collective-permute-start = (bf16[2,96,1024]{2,1,0:T(8,128)(2,1)}, bf16[2,96,1024]{2,1,0:T(8,128)(2,1)S(1)}, u32[]{:S(2)}, u32[]{:S(2)}) collective-permute-start(bf16[2,96,1024]{2,1,0:T(8,128)(2,1)} %bitcast.13), channel_id=1, source_target_pairs={{0,1},{1,0},{2,3},{3,2},{4,5},{5,4},{6,7},{7,6},{8,9},{9,8},{10,11... | collective-permute-start | bytes 1179656 | tf_op jit(solution)/shard_map/ppermute | solution.py:323
  125.4 1.0 copy-start.7
  126.3 2.1 %copy-start.2 = (bf16[1024,96]{0,1:T(8,128)(2,1)S(1)}, bf16[1024,96]{0,1:T(8,128)(2,1)}, u32[]{:S(2)}) copy-start(bf16[1024,96]{0,1:T(8,128)(2,1)} %param.8) | copy-start | bytes 589828
  126.3 2.1 %copy-start.3 = (bf16[192,1024]{1,0:T(8,128)(2,1)S(1)}, bf16[192,1024]{1,0:T(8,128)(2,1)}, u32[]{:S(2)}) copy-start(bf16[192,1024]{1,0:T(8,128)(2,1)} %reduce-scatter.2.cloned.1.call-done) | copy-start | bytes 1179652
Sparse Core Ops, SparseCore 0:
  10.1 50.3 all-gather.1
  71.6 45.3 reduce-scatter.1

commit v5 on v4

--- a/solution.py
+++ b/solution.py
@@ -38,9 +38,9 @@
     return cdf + u * dens
 
 
-def backward_kernel(lengths, rows, w_t, weight, cot_t, film, error, q_init,
-                    part, moment, p_out,
-                    row_buf, wt_buf, w_buf, cot_buf, err_buf, z_buf, part_buf, m_buf, sems):
+def backward_kernel(lengths, rows, w_t, weight, cot_t, film, p_error, q_init,
+                    part, z_out, d_out, p_out,
+                    row_buf, wt_buf, w_buf, cot_buf, z_buf, part_buf, sems):
     width = rows.shape[0]
     rank = q_init.shape[0]
     samples = lengths.shape[0]
@@ -58,9 +58,9 @@
     get_rows += [fetch(rows.at[cut], row_buf.at[cut]) for cut in cuts[1:]]
     get_cot = fetch(cot_t, cot_buf)
     get_w = fetch(weight, w_buf)
-    get_error = fetch(error.at[0], err_buf)
 
     film_t = film[...].T
+    puts = []
     for c in range(CHUNKS):
         cut = slice(c * step, (c + 1) * step)
         get_rows[c].wait()
@@ -69,6 +69,7 @@
                 row_buf[cut, k * SEQ:(k + 1) * SEQ].astype(F32) * film_t[cut, k:k + 1]
                 + film_t[cut, samples + k:samples + k + 1]
             ).astype(BF)
+        puts.append(fetch(z_buf.at[cuts[c]], z_out.at[cuts[c]]))
     get_wt.wait()
     get_cot.wait()
     position = lax.broadcasted_iota(jnp.int32, (1, SEQ), 1)
@@ -82,26 +83,17 @@
         )
         halves.append((cot_buf[:, cols].astype(F32) * gelu_slope(u) * valid).astype(BF))
     d_pre = jnp.concatenate(halves, axis=1)
+    d_out[...] = d_pre
     get_w.wait()
-    puts = []
     for c in range(CHUNKS):
         cut = slice(c * step, (c + 1) * step)
         part_buf[cut, :] = mm(w_buf[cut, :], d_pre, NN).astype(BF)
         puts.append(fetch(part_buf.at[cuts[c]], part.at[cuts[c]]))
-    get_error.wait()
     q_hi, q_lo = split(q_init[...])
-    q_both = jnp.concatenate([q_hi, q_lo], axis=0)
-    p_parts = []
-    for c in range(CHUNKS):
-        cut = slice(c * step, (c + 1) * step)
-        total = mm(z_buf[cut, :], d_pre, NT) + err_buf[cut, :].astype(F32)
-        m_buf[cut, :] = total
-        puts.append(fetch(m_buf.at[cuts[c]], moment.at[cuts[c]]))
-        m_hi, m_lo = split(total)
-        first = mm(q_both, m_hi, NT)
-        p = first[:rank] + first[rank:] + mm(q_hi, m_lo, NT)
-        p_parts.append(p)
-    p = jnp.concatenate(p_parts, axis=1)
+    qd = mm(jnp.concatenate([q_hi, q_lo], axis=0), d_pre, NN)
+    s_hi, s_lo = split(qd[:rank] + qd[rank:])
+    both = mm(jnp.concatenate([s_hi, s_lo], axis=0), z_buf[...], NT)
+    p = both[:rank] + both[rank:] + p_error[...]
     half = width // 2
     for k in range(rank):
         p_out[k] = jnp.concatenate([p[k:k + 1, :half], p[k:k + 1, half:]], axis=0).astype(BF)
@@ -109,17 +101,18 @@
         put.wait()
 
 
-def backward(lengths, rows, w_t, weight, cot_t, film, error, q_init):
+def backward(lengths, rows, w_t, weight, cot_t, film, p_error, q_init):
     width, tokens = rows.shape
     rank, hidden = q_init.shape
     return pl.pallas_call(
         backward_kernel,
         in_specs=[pl.BlockSpec(memory_space=pltpu.SMEM)]
-        + [IN_HBM] * 4 + [IN_VMEM, IN_HBM, IN_VMEM],
-        out_specs=[IN_HBM, IN_HBM, IN_VMEM],
+        + [IN_HBM] * 4 + [IN_VMEM] * 3,
+        out_specs=[IN_HBM, IN_HBM, IN_VMEM, IN_VMEM],
         out_shape=[
             jax.ShapeDtypeStruct((width, tokens), BF),
-            jax.ShapeDtypeStruct((width, hidden), F32),
+            jax.ShapeDtypeStruct((width, tokens), BF),
+            jax.ShapeDtypeStruct((hidden, tokens), BF),
             jax.ShapeDtypeStruct((rank, 2, width // 2), BF),
         ],
         scratch_shapes=[
@@ -127,17 +120,60 @@
             pltpu.VMEM((hidden, width), BF),
             pltpu.VMEM((width, hidden), BF),
             pltpu.VMEM((hidden, tokens), BF),
-            pltpu.VMEM((width, hidden), BF),
             pltpu.VMEM((width, tokens), BF),
             pltpu.VMEM((width, tokens), BF),
-            pltpu.VMEM((width, hidden), F32),
-            pltpu.SemaphoreType.DMA((3 * CHUNKS + 4,)),
+            pltpu.SemaphoreType.DMA((3 * CHUNKS + 3,)),
         ],
         compiler_params=pltpu.CompilerParams(vmem_limit_bytes=50 * MIB),
         cost_estimate=pl.CostEstimate(
-            flops=6 * tokens * width * hidden, bytes_accessed=14 * MIB, transcendentals=0
-        ),
-    )(lengths, rows, w_t, weight, cot_t, film, error, q_init)
+            flops=10_000_000_000, bytes_accessed=14 * MIB, transcendentals=0
+        ),
+    )(lengths, rows, w_t, weight, cot_t, film, p_error, q_init)
+
+
+def error_kernel(error, q_init, out):
+    rank = q_init.shape[0]
+    q_hi, q_lo = split(q_init[...])
+    both = mm(jnp.concatenate([q_hi, q_lo], axis=0), error[0], NT)
+    out[...] = both[:rank] + both[rank:]
+
+
+def error_share(error, q_init):
+    rank, hidden = q_init.shape
+    width = error.shape[1]
+    return pl.pallas_call(
+        error_kernel,
+        out_shape=jax.ShapeDtypeStruct((rank, width), F32),
+        compiler_params=pltpu.CompilerParams(vmem_limit_bytes=16 * MIB),
+        cost_estimate=pl.CostEstimate(
+            flops=1_000_000_000, bytes_accessed=2 * MIB, transcendentals=0
+        ),
+    )(error, q_init)
+
+
+def moment_kernel(z, d_pre, error, out):
+    out[...] = mm(z[...], d_pre[...], NT) + error[0].astype(F32)
+
+
+def moment_of(z, d_pre, error):
+    width, tokens = z.shape
+    hidden = d_pre.shape[0]
+    step = width // CHUNKS
+    return pl.pallas_call(
+        moment_kernel,
+        grid=(CHUNKS,),
+        in_specs=[
+            pl.BlockSpec((step, tokens), lambda i: (i, 0)),
+            IN_VMEM,
+            pl.BlockSpec((1, step, hidden), lambda i: (0, i, 0)),
+        ],
+        out_specs=pl.BlockSpec((step, hidden), lambda i: (i, 0)),
+        out_shape=jax.ShapeDtypeStruct((width, hidden), F32),
+        compiler_params=pltpu.CompilerParams(vmem_limit_bytes=20 * MIB),
+        cost_estimate=pl.CostEstimate(
+            flops=3_500_000_000, bytes_accessed=6 * MIB, transcendentals=0
+        ),
+    )(z, d_pre, error)
 
 
 def right_kernel(p_rows, moment, y_out):
@@ -302,9 +338,11 @@
     start = lax.axis_index(TENSOR) * col_width
     own_scale = lax.dynamic_slice_in_dim(film_scale, start, col_width, 1).T
     film, own_scale = lax.optimization_barrier((film, own_scale))
-    part, moment, p_local = backward(
-        lengths, rows, weight.T, weight, cotangent.T, film, error, q_init
+    p_error = error_share(error, q_init)
+    part, z, d_pre, p_local = backward(
+        lengths, rows, weight.T, weight, cotangent.T, film, p_error, q_init
     )
+    moment = moment_of(z, d_pre, error)
 
     dz_pair = lax.psum_scatter(part, "z", scatter_dimension=0, tiled=True)
     dz_pair = dz_pair.reshape(2, col_width, -1)

time: 137 us -> 135 us (0.985)
  blocking collectives: 37.8 us -> 25.1 us
  local copies, waits for them, and re-layouts: 5.38 us -> 9.74 us
  starting transfers between devices: 9.31 us -> 13.6 us
    all_to_all x1 -> x0, blocking collectives: 12.6 us -> none  [local(): lax.all_to_all(jnp.broadcast_to(p_row[None], (replicas,) + p_row.shape),...]
    all_to_all x0 -> x1, starting transfers between devices: none -> 3.86 us  [local(): lax.all_to_all(jnp.broadcast_to(p_row[None], (replicas,) + p_row.shape),...]
    unnamed x19 -> x17, local copies, waits for them, and re-layouts: 3.86 us -> 7.57 us
    all_to_all x0 -> x1, waiting for transfers between devices: none -> 3.67 us  [local(): lax.all_to_all(jnp.broadcast_to(p_row[None], (replicas,) + p_row.shape),...]
    pallas_call x0 -> x2, Pallas kernels: none -> 2.67 us  [the longest x1 2.2 us: moment_of(): pl.pallas_call(moment_kernel, grid=(CHUNKS,), in_specs=[pl.BlockSpec((ste...]
    all_gather x1, waiting for transfers between devices: 48.8 us -> 46.2 us  [local(): rows = lax.all_gather(own, TENSOR, axis=0, tiled=True)]
    pallas_call x1, Pallas kernels: 10.8 us -> 8.6 us  [backward(): pl.pallas_call(backward_kernel, in_specs=[pl.BlockSpec(memory_space=pltpu...]
  transfers between devices with their start and end apart: 4 -> 5, of which waited for: 1 -> 2; matrix products, arithmetic and copies ran while one was open for 3% -> 5% of each run, Pallas kernels for 5% -> 7%
where the time goes in v5:
time: 135 us; the launch traced here: 134 us
  waiting for transfers between devices  50.6 us (37%)
  blocking collectives  25.1 us (19%)
  Pallas kernels  19.6 us (15%)
  between operations  14.2 us (11%)
  starting transfers between devices  13.6 us (10%)
  local copies, waits for them, and re-layouts  9.74 us (7%)
    all_gather x1, waiting for transfers between devices, local(): rows = lax.all_gather(own, TENSOR, axis=0, tiled=True)  46.2 us
    all_to_all x1, blocking collectives, local(): p_parts = lax.all_to_all(p_local, DP, 0, 0, tiled=True)  18.1 us
    pallas_call x1, Pallas kernels, backward(): pl.pallas_call(backward_kernel, in_specs=[pl.BlockSpec(memory_space=pltpu...  8.6 us
    unnamed x17, local copies, waits for them, and re-layouts  7.57 us
    all_to_all x1, blocking collectives, local(): lax.all_to_all(jnp.broadcast_to(y[None], (nx, rank, hidden)), 'x', 0, 0,...  7.03 us
    ppermute x1, starting transfers between devices, local(): dz_peer = lax.ppermute(dz_pair, 'core', SWAP)  5.54 us
    pallas_call x1, Pallas kernels, gram_schmidt(): pl.pallas_call(gram_schmidt_kernel, out_shape=[jax.ShapeDtypeStruct((rank...  4.66 us
    all_to_all x1, starting transfers between devices, local(): lax.all_to_all(jnp.broadcast_to(y[None], (ny, rank, hidden)), 'y', 0, 0,...  4.16 us
  transfers between devices with their start and end apart: 5, of which 2 were waited for; matrix products, arithmetic and copies ran while one was open for 5% of the time, Pallas kernels for 7%

profile of v5, /device:TPU:1, one launch (start us, length us, event | category | flops | bytes accessed | tf_op | source)
XLA Modules:
  0.0 133.7 jit_solution(17574028593713690119)
XLA Ops:
  7.2 0.0 all-gather.2.cloned.1.call-start
  7.2 0.7 all-gather.2.cloned.1.call-update
  7.9 0.0 reduce-scatter.2.cloned.1.call-start
  8.0 0.8 constant_dynamic-slice_fusion
  8.7 0.1 copy.20
  8.8 0.8 pad_maximum_fusion.film
  9.6 1.4 %copy.18 = bf16[1024,384]{0,1:T(8,128)(2,1)S(1)} copy(bf16[1024,384]{1,0:T(8,128)(2,1)} %param.9) | data formatting | bytes 1572864 | tf_op args[1]
  11.0 1.6 %copy.17 = bf16[1536,384]{0,1:T(8,128)(2,1)S(1)} copy(bf16[1536,384]{1,0:T(8,128)(2,1)} %weight.1) | data formatting | bytes 2359296 | tf_op args[2]
  12.6 0.0 copy-start.1
  12.6 1.3 copy-done.1
  13.9 0.5 shard_map.127.p_error
  14.4 46.2 %all-gather.2.cloned.1.call-done.rows = bf16[1536,1024]{1,0:T(8,128)(2,1)} async-done(((bf16[96,1024]{1,0:T(8,128)(2,1)}), bf16[1536,1024]{1,0:T(8,128)(2,1)}) %all-gather.2.cloned.1.call-update) | async-done | bytes 3145744 | tf_op jit(solution)/shard_map/all_gather | solution.py:335
  60.6 8.6 %shard_map.128 = (bf16[1536,1024]{1,0:T(8,128)(2,1)}, bf16[1536,1024]{1,0:T(8,128)(2,1)}, bf16[384,1024]{1,0:T(8,128)(2,1)S(1)}, bf16[32,2,768]{2,1,0:T(2,128)(2,1)S(1)}) custom-call(s32[4]{0:T(128)S(1)} %copy-done.5, bf16[1536,1024]{1,0:T(8,128)(2,1)} %all-gather.2.cloned.1.call-done.rows, bf16[384,1536]{1,0:T(8,128)(2,1)S(1)} %bitcast.8, ...), custom_call_target="tpu_custom_call" | custom-call | flops 10000000000 | bytes 14680064 | tf_op jit(solution)/shard_map/pallas_call | solution.py:107
  69.2 0.0 reduce-scatter.2.cloned.1.call-update
  69.2 18.1 %all_to_all.20 = bf16[32,2,768]{2,1,0:T(2,128)(2,1)S(1)} all-to-all(bf16[32,2,768]{2,1,0:T(2,128)(2,1)S(1)} %get-tuple-element.24), channel_id=1, replica_groups=mesh['x'=4,'y'=8,'z'=8,'core'=2] {'x','y'}, dimensions={0} | all-to-all | bytes 196608 | tf_op jit(solution)/shard_map/all_to_all | solution.py:349
  87.3 0.1 reduce_sum.24
  87.4 0.7 broadcast_in_dim.8
  88.1 3.9 %all-to-all-start.1 = ((bf16[32,2,768]{2,1,0:T(2,128)(2,1)}), bf16[32,2,768]{2,1,0:T(2,128)(2,1)S(1)}, u32[]{:S(2)}, u32[]{:S(2)}) async-start(bf16[32,2,768]{2,1,0:T(2,128)(2,1)} %broadcast_in_dim.8), calls=%async_computation.2 | async-start | bytes 196608 | tf_op jit(solution)/shard_map/all_to_all | solution.py:351
  91.9 0.0 copy-start.2
  92.0 1.3 copy-done.2
  93.2 1.9 %copy-done.6 = bf16[1536,1024]{1,0:T(8,128)(2,1)S(1)} copy-done((bf16[1536,1024]{1,0:T(8,128)(2,1)S(1)}, bf16[1536,1024]{1,0:T(8,128)(2,1)}, u32[]{:S(2)}) %copy-start.6) | copy-done | bytes 3145752
  95.2 2.2 %shard_map.129.moment = f32[1536,384]{1,0:T(8,128)S(1)} custom-call(bf16[1536,1024]{1,0:T(8,128)(2,1)S(1)} %copy-done.6, bf16[384,1024]{1,0:T(8,128)(2,1)S(1)} %get-tuple-element.26.d_pre, bf16[1,1536,384]{2,1,0:T(8,128)(2,1)S(1)} %copy-done.2), custom_call_target="tpu_custom_call" | custom-call | flops 3500000000 | bytes 6291456 | tf_op jit(solution)/shard_map/pallas_call | solution.py:162
  97.4 3.7 %all-to-all-done.1.p_rows = bf16[32,2,768]{2,1,0:T(2,128)(2,1)S(1)} async-done(((bf16[32,2,768]{2,1,0:T(2,128)(2,1)}), bf16[32,2,768]{2,1,0:T(2,128)(2,1)S(1)}, u32[]{:S(2)}, u32[]{:S(2)}) %all-to-all-start.1) | async-done | bytes 98336 | tf_op jit(solution)/shard_map/all_to_all | solution.py:351
  101.0 0.6 shard_map.130
  101.6 7.0 %all_to_all.21 = bf16[4,32,384]{2,1,0:T(8,128)(2,1)S(1)} all-to-all(bf16[4,32,384]{2,1,0:T(8,128)(2,1)S(1)} %broadcast_in_dim.9), channel_id=1, replica_groups=mesh['x'=4,'y'=8,'z'=8,'core'=2] {'x'}, dimensions={0} | all-to-all | bytes 196608 | tf_op jit(solution)/shard_map/all_to_all | solution.py:356
  108.7 0.7 broadcast_in_dim.11
  109.4 4.2 %all-to-all-start.3 = ((bf16[8,32,384]{2,1,0:T(8,128)(2,1)}), bf16[8,32,384]{2,1,0:T(8,128)(2,1)S(1)}, u32[]{:S(2)}, u32[]{:S(2)}) async-start(bf16[8,32,384]{2,1,0:T(8,128)(2,1)} %broadcast_in_dim.11), calls=%async_computation.4 | async-start | bytes 393216 | tf_op jit(solution)/shard_map/all_to_all | solution.py:365
  113.5 4.7 %shard_map.131 = (f32[32,1536]{1,0:T(8,128)}, f32[32,128]{1,0:T(8,128)S(1)}, bf16[96,1536]{1,0:T(8,128)(2,1)S(1)}) custom-call(bf16[32,2,768]{2,1,0:T(2,128)(2,1)S(1)} %all-to-all-done.1.p_rows), custom_call_target="tpu_custom_call" | custom-call | flops 5299999744 | bytes 1048576 | tf_op jit(solution)/shard_map/pallas_call | solution.py:234
  118.2 5.5 %collective-permute-start = (bf16[2,96,1024]{2,1,0:T(8,128)(2,1)}, bf16[2,96,1024]{2,1,0:T(8,128)(2,1)S(1)}, u32[]{:S(2)}, u32[]{:S(2)}) collective-permute-start(bf16[2,96,1024]{2,1,0:T(8,128)(2,1)} %bitcast.13), channel_id=1, source_target_pairs={{0,1},{1,0},{2,3},{3,2},{4,5},{5,4},{6,7},{7,6},{8,9},{9,8},{10,11... | collective-permute-start | bytes 1179656 | tf_op jit(solution)/shard_map/ppermute | solution.py:361
  123.8 0.0 copy-start
  123.8 2.1 %shard_map.133 = (f32[32,384]{1,0:T(8,128)}, bf16[1,1536,384]{2,1,0:T(8,128)(2,1)}) custom-call(bf16[8,32,384]{2,1,0:T(8,128)(2,1)S(1)} %all-to-all-done.3.y_parts, f32[32,128]{1,0:T(8,128)S(1)} %get-tuple-element.28.mix, bf16[96,1536]{1,0:T(8,128)(2,1)S(1)} %get-tuple-element.35.stack, f32[1536,384]{1,0:T(8,128)S(1)} %shard_map.129.moment), custom_call_target="tpu_custom_call" | custom-call | flops 2500000000 | bytes 4194304 | tf_op jit(solution)/shard_map/pallas_call | solution.py:278
  125.9 1.0 shard_map.132
  (13 shorter events, 0.1 us)
Async XLA Ops:
  7.2 5.4 %copy-start.4 = (f32[32,384]{1,0:T(8,128)S(1)}, f32[32,384]{1,0:T(8,128)}, u32[]{:S(2)}) copy-start(f32[32,384]{1,0:T(8,128)} %q_init.3) | copy-start | bytes 147460
  7.2 53.4 %all-gather.2.cloned.1.call-start = ((), (), s32[]{:S(2)}) async-start(), calls=%async_computation.5 | async-start | bytes 3342336 | tf_op jit(solution)/shard_map/all_gather | solution.py:335
  7.9 110.3 %reduce-scatter.2.cloned.1.call-start = ((), (), s32[]{:S(2)}) async-start(), calls=%async_computation.6 | async-start | bytes 3538944 | tf_op jit(solution)/shard_map/reduce_scatter | solution.py:347
  12.6 1.3 copy-start.1
  13.9 46.7 %copy-start.5 = (s32[4]{0:T(128)S(1)}, s32[4]{0:T(128)}, u32[]{:S(2)}) copy-start(s32[4]{0:T(128)} %lengths.1) | copy-start | bytes 52
  88.1 13.0 %all-to-all-start.1 = ((bf16[32,2,768]{2,1,0:T(2,128)(2,1)}), bf16[32,2,768]{2,1,0:T(2,128)(2,1)S(1)}, u32[]{:S(2)}, u32[]{:S(2)}) async-start(bf16[32,2,768]{2,1,0:T(2,128)(2,1)} %broadcast_in_dim.8), calls=%async_computation.2 | async-start | bytes 196608 | tf_op jit(solution)/shard_map/all_to_all | solution.py:351
  91.9 1.3 copy-start.2
  93.2 1.9 %copy-start.6 = (bf16[1536,1024]{1,0:T(8,128)(2,1)S(1)}, bf16[1536,1024]{1,0:T(8,128)(2,1)}, u32[]{:S(2)}) copy-start(bf16[1536,1024]{1,0:T(8,128)(2,1)} %get-tuple-element.25.z) | copy-start | bytes 9437188
  109.4 14.4 %all-to-all-start.3 = ((bf16[8,32,384]{2,1,0:T(8,128)(2,1)}), bf16[8,32,384]{2,1,0:T(8,128)(2,1)S(1)}, u32[]{:S(2)}, u32[]{:S(2)}) async-start(bf16[8,32,384]{2,1,0:T(8,128)(2,1)} %broadcast_in_dim.11), calls=%async_computation.4 | async-start | bytes 393216 | tf_op jit(solution)/shard_map/all_to_all | solution.py:365
  118.2 7.7 %collective-permute-start = (bf16[2,96,1024]{2,1,0:T(8,128)(2,1)}, bf16[2,96,1024]{2,1,0:T(8,128)(2,1)S(1)}, u32[]{:S(2)}, u32[]{:S(2)}) collective-permute-start(bf16[2,96,1024]{2,1,0:T(8,128)(2,1)} %bitcast.13), channel_id=1, source_target_pairs={{0,1},{1,0},{2,3},{3,2},{4,5},{5,4},{6,7},{7,6},{8,9},{9,8},{10,11... | collective-permute-start | bytes 1179656 | tf_op jit(solution)/shard_map/ppermute | solution.py:361
  123.8 2.1 %copy-start = (bf16[1024,96]{0,1:T(8,128)(2,1)S(1)}, bf16[1024,96]{0,1:T(8,128)(2,1)}, u32[]{:S(2)}) copy-start(bf16[1024,96]{0,1:T(8,128)(2,1)} %param.8) | copy-start | bytes 589828
  123.8 2.1 %copy-start.3 = (bf16[192,1024]{1,0:T(8,128)(2,1)S(1)}, bf16[192,1024]{1,0:T(8,128)(2,1)}, u32[]{:S(2)}) copy-start(bf16[192,1024]{1,0:T(8,128)(2,1)} %reduce-scatter.2.cloned.1.call-done) | copy-start | bytes 1179652
Sparse Core Ops, SparseCore 0:
  10.1 50.3 all-gather.1
  69.3 45.3 reduce-scatter.1

commit v6 on v5

--- a/solution.py
+++ b/solution.py
@@ -183,20 +183,42 @@
         [jnp.concatenate([row[h:h + 1] for row in rows], axis=0) for h in range(2)], axis=1
     ).astype(BF)
     m_hi, m_lo = split(moment[...])
-    y_out[...] = (mm(p, m_hi, NN) + mm(p, m_lo, NN)).astype(BF)
-
-
-def right_factor(p_rows, moment):
+    y = (mm(p, m_hi, NN) + mm(p, m_lo, NN)).astype(BF)
+    for k in range(y_out.shape[0]):
+        y_out[k] = y
+
+
+def right_factor(p_rows, moment, copies):
     rank = p_rows.shape[0]
     width, hidden = moment.shape
     return pl.pallas_call(
         right_kernel,
-        out_shape=jax.ShapeDtypeStruct((rank, hidden), BF),
+        out_shape=jax.ShapeDtypeStruct((copies, rank, hidden), BF),
         compiler_params=pltpu.CompilerParams(vmem_limit_bytes=32 * MIB),
         cost_estimate=pl.CostEstimate(
             flops=600_000_000, bytes_accessed=MIB, transcendentals=0
         ),
     )(p_rows, moment)
+
+
+def spread_kernel(parts, out):
+    total = parts[0].astype(F32)
+    for k in range(1, parts.shape[0]):
+        total = total + parts[k].astype(F32)
+    total = total.astype(BF)
+    for k in range(out.shape[0]):
+        out[k] = total
+
+
+def spread(parts, copies):
+    return pl.pallas_call(
+        spread_kernel,
+        out_shape=jax.ShapeDtypeStruct((copies,) + parts.shape[1:], BF),
+        compiler_params=pltpu.CompilerParams(vmem_limit_bytes=16 * MIB),
+        cost_estimate=pl.CostEstimate(
+            flops=400_000_000, bytes_accessed=MIB, transcendentals=0
+        ),
+    )(parts)
 
 
 def gram_schmidt_kernel(p_rows, basis_out, mix_out, stack_out, p, work):
@@ -347,14 +369,10 @@
     dz_pair = lax.psum_scatter(part, "z", scatter_dimension=0, tiled=True)
     dz_pair = dz_pair.reshape(2, col_width, -1)
     p_parts = lax.all_to_all(p_local, DP, 0, 0, tiled=True)
-    p_row = jnp.sum(p_parts.astype(F32), axis=0).astype(BF)
-    p_rows = lax.all_to_all(
-        jnp.broadcast_to(p_row[None], (replicas,) + p_row.shape), DP, 0, 0, tiled=True
-    )
-    y = right_factor(p_rows, moment)
+    p_rows = lax.all_to_all(spread(p_parts, replicas), DP, 0, 0, tiled=True)
     nx, ny = lax.axis_size("x"), lax.axis_size("y")
-    y_x = lax.all_to_all(jnp.broadcast_to(y[None], (nx, rank, hidden)), "x", 0, 0, tiled=True)
-    y = jnp.sum(y_x.astype(F32), axis=0).astype(BF)
+    y_x = lax.all_to_all(right_factor(p_rows, moment, nx), "x", 0, 0, tiled=True)
+    y = spread(y_x, ny)
     p_late, _ = lax.optimization_barrier((p_rows, y))
     basis, mix, stack = gram_schmidt(p_late)
     dz_pair, _ = lax.optimization_barrier((dz_pair, mix))
@@ -362,7 +380,7 @@
     d_normed, d_scale, d_shift = film_gradients(
         core.reshape(1), dz_pair, dz_peer, own, own_scale
     )
-    y_y = lax.all_to_all(jnp.broadcast_to(y[None], (ny, rank, hidden)), "y", 0, 0, tiled=True)
+    y_y = lax.all_to_all(y, "y", 0, 0, tiled=True)
     q_new, new_error = finish(replicas, y_y, mix, stack, moment)
     return (d_normed.T, d_scale, d_shift, basis[None], q_new, new_error)
 

time: 135 us -> 135 us (level)
  local copies, waits for them, and re-layouts: 9.74 us -> 8.34 us
  Pallas kernels: 19.6 us -> 21 us
    broadcast_in_dim x3 -> x0, local copies, waits for them, and re-layouts: 1.4 us -> none  [the longest x1 0.7 us: local(): jnp.broadcast_to(p_row[None], (replicas,) + p_row.shape)]
    pallas_call x1 -> x3, Pallas kernels: 0.58 us -> 1.97 us  [the longest x2 1.39 us: spread(): pl.pallas_call(spread_kernel, out_shape=jax.ShapeDtypeStruct((copies,) +...]
  transfers between devices with their start and end apart: 5 -> 5, of which waited for: 2 -> 2; matrix products, arithmetic and copies ran while one was open for 5% -> 3% of each run, Pallas kernels for 7% -> 9%
where the time goes in v6:
time: 135 us; the launch traced here: 134 us
  waiting for transfers between devices  50.6 us (37%)
  blocking collectives  25.1 us (19%)
  Pallas kernels  21 us (16%)
  between operations  14.2 us (11%)
  starting transfers between devices  13.6 us (10%)
  local copies, waits for them, and re-layouts  8.34 us (6%)
    all_gather x1, waiting for transfers between devices, local(): rows = lax.all_gather(own, TENSOR, axis=0, tiled=True)  46.2 us
    all_to_all x1, blocking collectives, local(): p_parts = lax.all_to_all(p_local, DP, 0, 0, tiled=True)  18.1 us
    pallas_call x1, Pallas kernels, backward(): pl.pallas_call(backward_kernel, in_specs=[pl.BlockSpec(memory_space=pltpu...  8.6 us
    unnamed x17, local copies, waits for them, and re-layouts  7.57 us
    all_to_all x1, blocking collectives, local(): lax.all_to_all(right_factor(p_rows, moment, nx), 'x', 0, 0, tiled=True)  7.03 us
    ppermute x1, starting transfers between devices, local(): dz_peer = lax.ppermute(dz_pair, 'core', SWAP)  5.54 us
    pallas_call x1, Pallas kernels, gram_schmidt(): pl.pallas_call(gram_schmidt_kernel, out_shape=[jax.ShapeDtypeStruct((rank...  4.66 us
    all_to_all x1, starting transfers between devices, local(): y_y = lax.all_to_all(y, 'y', 0, 0, tiled=True)  4.16 us
  transfers between devices with their start and end apart: 5, of which 2 were waited for; matrix products, arithmetic and copies ran while one was open for 3% of the time, Pallas kernels for 9%

profile of v6, /device:TPU:1, one launch (start us, length us, event | category | flops | bytes accessed | tf_op | source)
XLA Modules:
  0.0 133.6 jit_solution(15174140869659800595)
XLA Ops:
  7.2 0.0 all-gather.2.cloned.1.call-start
  7.2 0.7 all-gather.2.cloned.1.call-update
  7.9 0.0 reduce-scatter.2.cloned.1.call-start
  8.0 0.8 constant_dynamic-slice_fusion
  8.7 0.1 copy.17
  8.8 0.8 pad_maximum_fusion.film
  9.6 1.4 %copy.15 = bf16[1024,384]{0,1:T(8,128)(2,1)S(1)} copy(bf16[1024,384]{1,0:T(8,128)(2,1)} %param.9) | data formatting | bytes 1572864 | tf_op args[1]
  11.0 1.6 %copy.14 = bf16[1536,384]{0,1:T(8,128)(2,1)S(1)} copy(bf16[1536,384]{1,0:T(8,128)(2,1)} %weight.1) | data formatting | bytes 2359296 | tf_op args[2]
  12.6 0.0 copy-start.1
  12.6 1.3 copy-done.1
  13.9 0.5 shard_map.127.p_error
  14.4 46.2 %all-gather.2.cloned.1.call-done.rows = bf16[1536,1024]{1,0:T(8,128)(2,1)} async-done(((bf16[96,1024]{1,0:T(8,128)(2,1)}), bf16[1536,1024]{1,0:T(8,128)(2,1)}) %all-gather.2.cloned.1.call-update) | async-done | bytes 3145744 | tf_op jit(solution)/shard_map/all_gather | solution.py:357
  60.6 8.6 %shard_map.128 = (bf16[1536,1024]{1,0:T(8,128)(2,1)}, bf16[1536,1024]{1,0:T(8,128)(2,1)}, bf16[384,1024]{1,0:T(8,128)(2,1)S(1)}, bf16[32,2,768]{2,1,0:T(2,128)(2,1)S(1)}) custom-call(s32[4]{0:T(128)S(1)} %copy-done.5, bf16[1536,1024]{1,0:T(8,128)(2,1)} %all-gather.2.cloned.1.call-done.rows, bf16[384,1536]{1,0:T(8,128)(2,1)S(1)} %bitcast.8, ...), custom_call_target="tpu_custom_call" | custom-call | flops 10000000000 | bytes 14680064 | tf_op jit(solution)/shard_map/pallas_call | solution.py:107
  69.2 0.0 reduce-scatter.2.cloned.1.call-update
  69.2 18.1 %all_to_all.20.parts = bf16[32,2,768]{2,1,0:T(2,128)(2,1)S(1)} all-to-all(bf16[32,2,768]{2,1,0:T(2,128)(2,1)S(1)} %get-tuple-element.24), channel_id=1, replica_groups=mesh['x'=4,'y'=8,'z'=8,'core'=2] {'x','y'}, dimensions={0} | all-to-all | bytes 196608 | tf_op jit(solution)/shard_map/all_to_all | solution.py:371
  87.3 0.7 shard_map.129
  88.0 3.9 %all-to-all-start.1 = ((bf16[32,2,768]{2,1,0:T(2,128)(2,1)}), bf16[32,2,768]{2,1,0:T(2,128)(2,1)S(1)}, u32[]{:S(2)}, u32[]{:S(2)}) async-start(bf16[32,2,768]{2,1,0:T(2,128)(2,1)} %shard_map.129), calls=%async_computation.2 | async-start | bytes 196608 | tf_op jit(solution)/shard_map/all_to_all | solution.py:372
  91.8 0.0 copy-start.2
  91.8 1.3 copy-done.2
  93.1 1.9 %copy-done.6 = bf16[1536,1024]{1,0:T(8,128)(2,1)S(1)} copy-done((bf16[1536,1024]{1,0:T(8,128)(2,1)S(1)}, bf16[1536,1024]{1,0:T(8,128)(2,1)}, u32[]{:S(2)}) %copy-start.6) | copy-done | bytes 3145752
  95.0 2.2 %shard_map.130.moment = f32[1536,384]{1,0:T(8,128)S(1)} custom-call(bf16[1536,1024]{1,0:T(8,128)(2,1)S(1)} %copy-done.6, bf16[384,1024]{1,0:T(8,128)(2,1)S(1)} %get-tuple-element.26.d_pre, bf16[1,1536,384]{2,1,0:T(8,128)(2,1)S(1)} %copy-done.2), custom_call_target="tpu_custom_call" | custom-call | flops 3500000000 | bytes 6291456 | tf_op jit(solution)/shard_map/pallas_call | solution.py:162
  97.3 3.7 %all-to-all-done.1.p_rows = bf16[32,2,768]{2,1,0:T(2,128)(2,1)S(1)} async-done(((bf16[32,2,768]{2,1,0:T(2,128)(2,1)}), bf16[32,2,768]{2,1,0:T(2,128)(2,1)S(1)}, u32[]{:S(2)}, u32[]{:S(2)}) %all-to-all-start.1) | async-done | bytes 98336 | tf_op jit(solution)/shard_map/all_to_all | solution.py:372
  100.9 0.6 shard_map.131
  101.5 7.0 %all_to_all.21.parts = bf16[4,32,384]{2,1,0:T(8,128)(2,1)S(1)} all-to-all(bf16[4,32,384]{2,1,0:T(8,128)(2,1)S(1)} %shard_map.131), channel_id=1, replica_groups=mesh['x'=4,'y'=8,'z'=8,'core'=2] {'x'}, dimensions={0} | all-to-all | bytes 196608 | tf_op jit(solution)/shard_map/all_to_all | solution.py:374
  108.6 0.7 shard_map.132
  109.2 4.2 %all-to-all-start.3 = ((bf16[8,32,384]{2,1,0:T(8,128)(2,1)}), bf16[8,32,384]{2,1,0:T(8,128)(2,1)S(1)}, u32[]{:S(2)}, u32[]{:S(2)}) async-start(bf16[8,32,384]{2,1,0:T(8,128)(2,1)} %shard_map.132), calls=%async_computation.4 | async-start | bytes 393216 | tf_op jit(solution)/shard_map/all_to_all | solution.py:383
  113.4 4.7 %shard_map.133 = (f32[32,1536]{1,0:T(8,128)}, f32[32,128]{1,0:T(8,128)S(1)}, bf16[96,1536]{1,0:T(8,128)(2,1)S(1)}) custom-call(bf16[32,2,768]{2,1,0:T(2,128)(2,1)S(1)} %all-to-all-done.1.p_rows), custom_call_target="tpu_custom_call" | custom-call | flops 5299999744 | bytes 1048576 | tf_op jit(solution)/shard_map/pallas_call | solution.py:256
  118.1 5.5 %collective-permute-start = (bf16[2,96,1024]{2,1,0:T(8,128)(2,1)}, bf16[2,96,1024]{2,1,0:T(8,128)(2,1)S(1)}, u32[]{:S(2)}, u32[]{:S(2)}) collective-permute-start(bf16[2,96,1024]{2,1,0:T(8,128)(2,1)} %bitcast.13), channel_id=1, source_target_pairs={{0,1},{1,0},{2,3},{3,2},{4,5},{5,4},{6,7},{7,6},{8,9},{9,8},{10,11... | collective-permute-start | bytes 1179656 | tf_op jit(solution)/shard_map/ppermute | solution.py:379
  123.6 0.0 copy-start
  123.7 2.1 %shard_map.135 = (f32[32,384]{1,0:T(8,128)}, bf16[1,1536,384]{2,1,0:T(8,128)(2,1)}) custom-call(bf16[8,32,384]{2,1,0:T(8,128)(2,1)S(1)} %all-to-all-done.3.y_parts, f32[32,128]{1,0:T(8,128)S(1)} %get-tuple-element.28.mix, bf16[96,1536]{1,0:T(8,128)(2,1)S(1)} %get-tuple-element.35.stack, f32[1536,384]{1,0:T(8,128)S(1)} %shard_map.130.moment), custom_call_target="tpu_custom_call" | custom-call | flops 2500000000 | bytes 4194304 | tf_op jit(solution)/shard_map/pallas_call | solution.py:300
  125.7 0.0 collective-permute-done.dz_peer
  125.8 1.0 shard_map.134
  (10 shorter events, 0.0 us)
Async XLA Ops:
  7.2 5.4 %copy-start.4 = (f32[32,384]{1,0:T(8,128)S(1)}, f32[32,384]{1,0:T(8,128)}, u32[]{:S(2)}) copy-start(f32[32,384]{1,0:T(8,128)} %q_init.3) | copy-start | bytes 147460
  7.2 53.4 %all-gather.2.cloned.1.call-start = ((), (), s32[]{:S(2)}) async-start(), calls=%async_computation.5 | async-start | bytes 3342336 | tf_op jit(solution)/shard_map/all_gather | solution.py:357
  7.9 110.2 %reduce-scatter.2.cloned.1.call-start = ((), (), s32[]{:S(2)}) async-start(), calls=%async_computation.6 | async-start | bytes 3538944 | tf_op jit(solution)/shard_map/reduce_scatter | solution.py:369
  12.6 1.3 copy-start.1
  13.9 46.7 %copy-start.5 = (s32[4]{0:T(128)S(1)}, s32[4]{0:T(128)}, u32[]{:S(2)}) copy-start(s32[4]{0:T(128)} %lengths.1) | copy-start | bytes 52
  88.0 13.0 %all-to-all-start.1 = ((bf16[32,2,768]{2,1,0:T(2,128)(2,1)}), bf16[32,2,768]{2,1,0:T(2,128)(2,1)S(1)}, u32[]{:S(2)}, u32[]{:S(2)}) async-start(bf16[32,2,768]{2,1,0:T(2,128)(2,1)} %shard_map.129), calls=%async_computation.2 | async-start | bytes 196608 | tf_op jit(solution)/shard_map/all_to_all | solution.py:372
  91.8 1.3 copy-start.2
  93.1 1.9 %copy-start.6 = (bf16[1536,1024]{1,0:T(8,128)(2,1)S(1)}, bf16[1536,1024]{1,0:T(8,128)(2,1)}, u32[]{:S(2)}) copy-start(bf16[1536,1024]{1,0:T(8,128)(2,1)} %get-tuple-element.25.z) | copy-start | bytes 9437188
  109.2 14.4 %all-to-all-start.3 = ((bf16[8,32,384]{2,1,0:T(8,128)(2,1)}), bf16[8,32,384]{2,1,0:T(8,128)(2,1)S(1)}, u32[]{:S(2)}, u32[]{:S(2)}) async-start(bf16[8,32,384]{2,1,0:T(8,128)(2,1)} %shard_map.132), calls=%async_computation.4 | async-start | bytes 393216 | tf_op jit(solution)/shard_map/all_to_all | solution.py:383
  118.1 7.7 %collective-permute-start = (bf16[2,96,1024]{2,1,0:T(8,128)(2,1)}, bf16[2,96,1024]{2,1,0:T(8,128)(2,1)S(1)}, u32[]{:S(2)}, u32[]{:S(2)}) collective-permute-start(bf16[2,96,1024]{2,1,0:T(8,128)(2,1)} %bitcast.13), channel_id=1, source_target_pairs={{0,1},{1,0},{2,3},{3,2},{4,5},{5,4},{6,7},{7,6},{8,9},{9,8},{10,11... | collective-permute-start | bytes 1179656 | tf_op jit(solution)/shard_map/ppermute | solution.py:379
  123.6 2.1 %copy-start = (bf16[1024,96]{0,1:T(8,128)(2,1)S(1)}, bf16[1024,96]{0,1:T(8,128)(2,1)}, u32[]{:S(2)}) copy-start(bf16[1024,96]{0,1:T(8,128)(2,1)} %param.8) | copy-start | bytes 589828
  123.6 2.1 %copy-start.3 = (bf16[192,1024]{1,0:T(8,128)(2,1)S(1)}, bf16[192,1024]{1,0:T(8,128)(2,1)}, u32[]{:S(2)}) copy-start(bf16[192,1024]{1,0:T(8,128)(2,1)} %reduce-scatter.2.cloned.1.call-done) | copy-start | bytes 1179652
Sparse Core Ops, SparseCore 0:
  10.1 50.3 all-gather.1
  69.3 45.3 reduce-scatter.1
